TPU v7x, 32 devices: a whole 2x2x4 slice. The times are simulated.
32 devices in a mesh: dp: 4 (over z), mp: 8 (over y, x, core).
Axes of the slice: x: 2, y: 2, z: 4, core: 2. Of those that a mesh axis runs over, the one named last changes fastest.
Arguments:
- tokens: bfloat16 [1024, 8192], P('dp', 'mp'), may hold values from -6 to 6
- router_weight: bfloat16 [8192, 64], P('mp'), may hold values from -0.0625 to 0.0625
- gate_cotangent: float32 [1024, 2], P('dp'), may hold values from -6 to 6
- expert_index: int32 [1024, 2], P('dp'), may hold values from 0 to 63, as said below
- slot_index: int32 [1024, 2], P('dp'), may hold values from -1 to 9, as said below
Outputs:
- gates: float32 [1024, 2], P(('dp', 'mp'))
- router_grad: float32 [8192, 64], P('mp')
- dispatched: bfloat16 [4, 64, 10, 8192], P('dp', 'mp')
Inputs may be any that keep to these rules, and one draw needn't show every extreme that they name: `expert_index`: the two picks of a token are different experts. `slot_index`: for each group, the picks are ranked per expert with all first picks in token order before all second picks in token order; a pick's slot is its rank if that is below 10, else -1. In every group some expert is picked more than 10 times, so its 10 slots are all filled.
All inputs are finite; a program needn't handle non-finite values.
Results may differ from a plain program's by a relative error of at most 0.0029.
Values may be sent and summed in bfloat16 or wider, within the bound.
A program may use at most 64 MiB of HBM per device.

v0:
```python
import jax
import jax.numpy as jnp
from jax import lax
from jax.sharding import PartitionSpec as P

balance_weight = 0.5
zloss_weight = 0.02


def route_grad(logits, cotangent, picks, load):
    levels = jnp.arange(logits.shape[1], dtype=jnp.int32)
    expo = jnp.exp(logits)
    total = jnp.sum(expo, axis=1, keepdims=True)
    probs = expo / total
    lse = jnp.log(total)
    first = (picks[:, 0:1] == levels[None, :]).astype(jnp.float32)
    second = (picks[:, 1:2] == levels[None, :]).astype(jnp.float32)
    pfirst = jnp.sum(probs * first, axis=1, keepdims=True)
    psecond = jnp.sum(probs * second, axis=1, keepdims=True)
    denom = pfirst + psecond
    gfirst = pfirst / denom
    gsecond = psecond / denom
    cfirst = cotangent[:, 0:1]
    csecond = cotangent[:, 1:2]
    mixed = cfirst * gfirst + csecond * gsecond
    upward = (
        first * (cfirst - mixed) / denom
        + second * (csecond - mixed) / denom
        + balance_weight * load[None, :]
    )
    inner = jnp.sum(probs * upward, axis=1, keepdims=True)
    grad = probs * (upward - inner) + 2.0 * zloss_weight * lse * probs
    gates = jnp.concatenate([gfirst, gsecond], axis=1)
    return (gates, grad.astype(jnp.bfloat16))


def on_device(tokens, router_weight, gate_cotangent, expert_index, slot_index):
    rows = tokens.shape[0]
    experts = router_weight.shape[1]
    owners = lax.axis_size("mp")
    own_rows = rows // owners
    capacity = 5 * rows // (2 * experts)
    levels = jnp.arange(experts, dtype=jnp.int32)
    local_counts = jnp.sum(
        (expert_index[:, :, None] == levels[None, None, :]).astype(jnp.float32), axis=(0, 1)
    )
    counts = lax.psum(local_counts, "dp")
    load = counts * experts / (2.0 * rows * lax.axis_size("dp"))
    cell = jnp.where(slot_index >= 0, expert_index * capacity + slot_index, -1)
    per_block = 8
    width = per_block * capacity

    def fill_block(block):
        targets = block * width + jnp.arange(width, dtype=jnp.int32)
        hits = (cell[:, 0:1] == targets[None, :]) | (cell[:, 1:2] == targets[None, :])
        onehot = hits.astype(jnp.bfloat16)
        placed = lax.dot_general(
            onehot, tokens, (((0,), (0,)), ((), ())), preferred_element_type=jnp.float32
        )
        return placed.astype(jnp.bfloat16)

    slotted = lax.map(fill_block, jnp.arange(experts // per_block, dtype=jnp.int32))
    slotted = slotted.reshape(experts, capacity, tokens.shape[1])
    received = lax.all_to_all(slotted, "mp", split_axis=0, concat_axis=2, tiled=True)
    dispatched = received[None]
    partial_value = jnp.dot(tokens, router_weight, preferred_element_type=jnp.float32)
    start = lax.axis_index("mp") * own_rows
    logits = lax.psum_scatter(partial_value, "mp", scatter_dimension=0, tiled=True)
    own_cot = lax.dynamic_slice_in_dim(gate_cotangent, start, own_rows, 0)
    own_picks = lax.dynamic_slice_in_dim(expert_index, start, own_rows, 0)
    gates, own_grad = route_grad(logits, own_cot, own_picks, load)
    grad_rows = lax.all_gather(own_grad, "mp", axis=0, tiled=True)
    weight_part = lax.dot_general(
        tokens, grad_rows, (((0,), (0,)), ((), ())), preferred_element_type=jnp.float32
    )
    router_grad = lax.psum(weight_part, "dp")
    return (gates, router_grad, dispatched)


def solution(mesh):
    in_specs = (P("dp", "mp"), P("mp", None), P("dp", None), P("dp", None), P("dp", None))
    out_specs = (P(("dp", "mp"), None), P("mp", None), P("dp", "mp", None, None))
    return jax.shard_map(
        on_device, mesh=mesh, in_specs=in_specs, out_specs=out_specs, check_vma=False
    )
```

profile of v0, /device:TPU:0, one launch (start us, length us, event | category | flops | bytes accessed | tf_op | source)
XLA Modules:
  0.0 114.6 jit_solution(4287249506631239027)
XLA Ops:
  7.2 0.0 copy-start
  7.2 0.0 reduce-scatter.2.cloned.1.call-start
  7.2 0.8 copy-done
  8.1 2.0 %fusion.9 = f32[256,64]{1,0:T(8,128)} fusion(bf16[256,1024]{1,0:T(8,128)(2,1)} %param.7, bf16[1024,64]{0,1:T(8,128)(2,1)S(1)} %copy-done), kind=kOutput, calls=%fused_computation.36 | convolution fusion | flops 33554432 | bytes 720896 | tf_op jit(solution)/shard_map/dot_general | solution.py:66
  10.1 0.0 reduce-scatter.2.cloned.1.call-update
  10.1 0.7 compare_select_fusion
  10.8 21.4 %while.10 = (s32[]{:T(128)}, bf16[8,80,1024]{2,1,0:T(8,128)(2,1)S(1)}, s32[256,2]{0,1:T(2,128)S(1)}, s32[8]{0:T(128)S(1)}, bf16[256,1024]{1,0:T(8,128)(2,1)}, /*index=5*/s32[]{:T(128)}, s32[1]{0:T(128)}) while((s32[]{:T(128)}, bf16[8,80,1024]{2,1,0:T(8,128)(2,1)S(1)}, s32[256,2]{0,1:T(2,128)S(1)}, s32[8]{0:T(128)S(1)}, ...), condition=%wide.region_9.10_spmd, body=%wide.region_8.9_spmd.sunk | while | flops 42086480 | bytes 695221 | solution.py:62
  10.8 0.6 dynamic_slice.15
  12.1 1.4 %fusion.22 = bf16[8,80,1024]{2,1,0:T(8,128)(2,1)S(1)} fusion(bf16[8,80,1024]{2,1,0:T(8,128)(2,1)S(1)} %get-tuple-element.94, s32[]{:T(128)S(6)} %copy.17, bf16[256,1024]{1,0:T(8,128)(2,1)} %get-tuple-element.104, s32[80]{0:T(128)S(1)} %iota_add_fusion.2, s32[256]{0:T(256)S(1)} %bitcast.49, s32[256]{0:T(256)S(1)} %bitcast.48), kind=kOutput, calls=%fused_computation.2.clone.1 | convolution fusion | flops 42086400 | bytes 690692 | tf_op jit(solution)/shard_map/while/body/eval_jaxpr/dot_general | solution.py:57
  13.5 0.6 dynamic_slice.15
  14.7 1.4 %fusion.22 = bf16[8,80,1024]{2,1,0:T(8,128)(2,1)S(1)} fusion(bf16[8,80,1024]{2,1,0:T(8,128)(2,1)S(1)} %get-tuple-element.94, s32[]{:T(128)S(6)} %copy.17, bf16[256,1024]{1,0:T(8,128)(2,1)} %get-tuple-element.104, s32[80]{0:T(128)S(1)} %iota_add_fusion.2, s32[256]{0:T(256)S(1)} %bitcast.49, s32[256]{0:T(256)S(1)} %bitcast.48), kind=kOutput, calls=%fused_computation.2.clone.1 | convolution fusion | flops 42086400 | bytes 690692 | tf_op jit(solution)/shard_map/while/body/eval_jaxpr/dot_general | solution.py:57
  16.2 0.6 dynamic_slice.15
  17.4 1.4 %fusion.22 = bf16[8,80,1024]{2,1,0:T(8,128)(2,1)S(1)} fusion(bf16[8,80,1024]{2,1,0:T(8,128)(2,1)S(1)} %get-tuple-element.94, s32[]{:T(128)S(6)} %copy.17, bf16[256,1024]{1,0:T(8,128)(2,1)} %get-tuple-element.104, s32[80]{0:T(128)S(1)} %iota_add_fusion.2, s32[256]{0:T(256)S(1)} %bitcast.49, s32[256]{0:T(256)S(1)} %bitcast.48), kind=kOutput, calls=%fused_computation.2.clone.1 | convolution fusion | flops 42086400 | bytes 690692 | tf_op jit(solution)/shard_map/while/body/eval_jaxpr/dot_general | solution.py:57
  18.8 0.6 dynamic_slice.15
  20.1 1.4 %fusion.22 = bf16[8,80,1024]{2,1,0:T(8,128)(2,1)S(1)} fusion(bf16[8,80,1024]{2,1,0:T(8,128)(2,1)S(1)} %get-tuple-element.94, s32[]{:T(128)S(6)} %copy.17, bf16[256,1024]{1,0:T(8,128)(2,1)} %get-tuple-element.104, s32[80]{0:T(128)S(1)} %iota_add_fusion.2, s32[256]{0:T(256)S(1)} %bitcast.49, s32[256]{0:T(256)S(1)} %bitcast.48), kind=kOutput, calls=%fused_computation.2.clone.1 | convolution fusion | flops 42086400 | bytes 690692 | tf_op jit(solution)/shard_map/while/body/eval_jaxpr/dot_general | solution.py:57
  21.5 0.6 dynamic_slice.15
  22.8 1.4 %fusion.22 = bf16[8,80,1024]{2,1,0:T(8,128)(2,1)S(1)} fusion(bf16[8,80,1024]{2,1,0:T(8,128)(2,1)S(1)} %get-tuple-element.94, s32[]{:T(128)S(6)} %copy.17, bf16[256,1024]{1,0:T(8,128)(2,1)} %get-tuple-element.104, s32[80]{0:T(128)S(1)} %iota_add_fusion.2, s32[256]{0:T(256)S(1)} %bitcast.49, s32[256]{0:T(256)S(1)} %bitcast.48), kind=kOutput, calls=%fused_computation.2.clone.1 | convolution fusion | flops 42086400 | bytes 690692 | tf_op jit(solution)/shard_map/while/body/eval_jaxpr/dot_general | solution.py:57
  24.2 0.6 dynamic_slice.15
  25.4 1.4 %fusion.22 = bf16[8,80,1024]{2,1,0:T(8,128)(2,1)S(1)} fusion(bf16[8,80,1024]{2,1,0:T(8,128)(2,1)S(1)} %get-tuple-element.94, s32[]{:T(128)S(6)} %copy.17, bf16[256,1024]{1,0:T(8,128)(2,1)} %get-tuple-element.104, s32[80]{0:T(128)S(1)} %iota_add_fusion.2, s32[256]{0:T(256)S(1)} %bitcast.49, s32[256]{0:T(256)S(1)} %bitcast.48), kind=kOutput, calls=%fused_computation.2.clone.1 | convolution fusion | flops 42086400 | bytes 690692 | tf_op jit(solution)/shard_map/while/body/eval_jaxpr/dot_general | solution.py:57
  26.9 0.6 dynamic_slice.15
  28.1 1.4 %fusion.22 = bf16[8,80,1024]{2,1,0:T(8,128)(2,1)S(1)} fusion(bf16[8,80,1024]{2,1,0:T(8,128)(2,1)S(1)} %get-tuple-element.94, s32[]{:T(128)S(6)} %copy.17, bf16[256,1024]{1,0:T(8,128)(2,1)} %get-tuple-element.104, s32[80]{0:T(128)S(1)} %iota_add_fusion.2, s32[256]{0:T(256)S(1)} %bitcast.49, s32[256]{0:T(256)S(1)} %bitcast.48), kind=kOutput, calls=%fused_computation.2.clone.1 | convolution fusion | flops 42086400 | bytes 690692 | tf_op jit(solution)/shard_map/while/body/eval_jaxpr/dot_general | solution.py:57
  29.5 0.6 dynamic_slice.15
  30.8 1.4 %fusion.22 = bf16[8,80,1024]{2,1,0:T(8,128)(2,1)S(1)} fusion(bf16[8,80,1024]{2,1,0:T(8,128)(2,1)S(1)} %get-tuple-element.94, s32[]{:T(128)S(6)} %copy.17, bf16[256,1024]{1,0:T(8,128)(2,1)} %get-tuple-element.104, s32[80]{0:T(128)S(1)} %iota_add_fusion.2, s32[256]{0:T(256)S(1)} %bitcast.49, s32[256]{0:T(256)S(1)} %bitcast.48), kind=kOutput, calls=%fused_computation.2.clone.1 | convolution fusion | flops 42086400 | bytes 690692 | tf_op jit(solution)/shard_map/while/body/eval_jaxpr/dot_general | solution.py:57
  32.2 1.6 %reshape.59 = bf16[64,10,1024]{2,1,0:T(8,128)(2,1)} reshape(bf16[8,80,1024]{2,1,0:T(8,128)(2,1)S(1)} %get-tuple-element.30) | data formatting | bytes 2621440 | tf_op jit(solution)/shard_map/reshape | solution.py:63
  33.8 0.0 copy-start.2
  33.8 0.0 copy-start.3
  33.8 0.0 copy-start.1
  33.8 5.3 %all-to-all-start = ((bf16[64,10,1024]{2,1,0:T(8,128)(2,1)}), bf16[64,10,1024]{2,1,0:T(8,128)(2,1)S(1)}, u32[]{:S(2)}, u32[]{:S(2)}) async-start(bf16[64,10,1024]{2,1,0:T(8,128)(2,1)} %reshape.59), calls=%async_computation.1 | async-start | bytes 4194304 | tf_op jit(solution)/shard_map/all_to_all | solution.py:64
  39.1 0.0 all-reduce.2.cloned.1.call-start
  39.2 0.0 copy-done.2
  39.2 0.1 convert_reduce_fusion
  39.3 12.0 %psum.14 = f32[64]{0:T(128)S(1)} all-reduce(f32[64]{0:T(128)S(1)} %convert_reduce_fusion), channel_id=1, replica_groups=mesh['dp'=4,'mp'=8] {'dp'}, use_global_device_ids=true, to_apply=%region_5.6 | all-reduce | flops 64 | bytes 512 | tf_op jit(solution)/shard_map/psum | solution.py:47
  51.3 0.1 constant_dynamic-slice_fusion.1
  51.3 0.0 copy-done.3
  51.3 0.1 constant_dynamic-slice_fusion
  51.4 0.8 exponential_reduce_fusion
  52.2 0.9 select_reduce_fusion.1
  53.2 0.9 multiply_reduce_fusion
  54.1 0.8 multiply_convert_fusion
  55.0 14.4 %all_gather.3 = bf16[256,64]{1,0:T(8,128)(2,1)S(1)} all-gather(bf16[32,64]{1,0:T(8,128)(2,1)S(1)} %multiply_convert_fusion), channel_id=1, replica_groups=mesh['dp'=4,'mp'=8] {'mp'}, dimensions={0}, use_global_device_ids=true | all-gather | bytes 36864 | tf_op jit(solution)/shard_map/all_gather | solution.py:72
  69.3 0.0 copy-done.1
  69.3 0.9 convolution_bitcast_fusion
  70.3 0.0 all-reduce.2.cloned.1.call-update
  70.3 0.6 pad_maximum_fusion
  70.9 0.0 all-to-all-done
  70.9 1.8 %copy.12 = bf16[8,10,8,1024]{3,0,2,1:T(8,128)(2,1)} copy(bf16[8,10,8,1024]{3,1,0,2:T(8,128)(2,1)S(1)} %bitcast.46) | data formatting | bytes 2621440 | tf_op jit(solution)/shard_map/all_to_all | solution.py:64
  72.7 33.4 %all-reduce.2.cloned.1.call-done = f32[1024,64]{0,1:T(8,128)} async-done(((f32[1024,64]{0,1:T(8,128)}), f32[1024,64]{0,1:T(8,128)}) %all-reduce.2.cloned.1.call-update) | async-done | bytes 262160 | tf_op jit(solution)/shard_map/psum | solution.py:76
  106.1 1.7 %copy.21 = f32[1024,64]{0,1:T(8,128)} copy(f32[1024,64]{0,1:T(8,128)} %all-reduce.2.cloned.1.call-done) | data formatting | bytes 524288
  (25 shorter events, 0.1 us)
Async XLA Ops:
  7.2 0.9 copy-start
  7.2 44.2 %reduce-scatter.2.cloned.1.call-start = ((), (), s32[]{:S(2)}) async-start(), calls=%async_computation.2 | async-start | bytes 147456 | tf_op jit(solution)/shard_map/reduce_scatter | solution.py:68
  33.8 5.4 %copy-start.2 = (s32[256,2]{0,1:T(2,128)S(1)}, s32[256,2]{0,1:T(2,128)}, u32[]{:S(2)}) copy-start(s32[256,2]{0,1:T(2,128)} %param.10) | copy-start | bytes 6148
  33.8 17.5 %copy-start.3 = (f32[256,2]{0,1:T(2,128)S(1)}, f32[256,2]{0,1:T(2,128)}, u32[]{:S(2)}) copy-start(f32[256,2]{0,1:T(2,128)} %param.9) | copy-start | bytes 6148
  33.8 35.5 %copy-start.1 = (bf16[256,1024]{1,0:T(8,128)(2,1)S(1)}, bf16[256,1024]{1,0:T(8,128)(2,1)}, u32[]{:S(2)}) copy-start(bf16[256,1024]{1,0:T(8,128)(2,1)} %get-tuple-element.112) | copy-start | bytes 1572868
  33.8 37.1 %all-to-all-start = ((bf16[64,10,1024]{2,1,0:T(8,128)(2,1)}), bf16[64,10,1024]{2,1,0:T(8,128)(2,1)S(1)}, u32[]{:S(2)}, u32[]{:S(2)}) async-start(bf16[64,10,1024]{2,1,0:T(8,128)(2,1)} %reshape.59), calls=%async_computation.1 | async-start | bytes 4194304 | tf_op jit(solution)/shard_map/all_to_all | solution.py:64
  39.1 67.0 %all-reduce.2.cloned.1.call-start = ((), (), s32[]{:S(2)}) async-start(), calls=%async_computation.3 | async-start | bytes 524288 | tf_op jit(solution)/shard_map/psum | solution.py:76
Sparse Core Ops, SparseCore 0:
  11.6 36.2 reduce-scatter.1
  70.4 35.6 all-reduce.1
where the time goes:
time: 116 us; the launch traced here: 115 us
  waiting for transfers between devices  33.5 us (29%)
  blocking collectives  26.4 us (23%)
  matrix products  14.1 us (12%)
  between operations  14.1 us (12%)
  local copies, waits for them, and re-layouts  10.8 us (9%)
  loops' own time  5.5 us (5%)
  starting transfers between devices  5.38 us (5%)
  other arithmetic  4.94 us (4%)
    psum x1, waiting for transfers between devices, on_device(): router_grad = lax.psum(weight_part, 'dp')  33.4 us
    all_gather x1, blocking collectives, on_device(): grad_rows = lax.all_gather(own_grad, 'mp', axis=0, tiled=True)  14.4 us
    psum x1, blocking collectives, on_device(): counts = lax.psum(local_counts, 'dp')  12 us
    dot_general x8, matrix products, fill_block(): lax.dot_general(onehot, tokens, (((0,), (0,)), ((), ())), preferred_eleme...  11.1 us
    another operation x1, loops' own time, on_device(): lax.map(fill_block, jnp.arange(experts // per_block, dtype=jnp.int32))  5.5 us
    all_to_all x1, starting transfers between devices, on_device(): lax.all_to_all(slotted, 'mp', split_axis=0, concat_axis=2, tiled=True)  5.31 us
    dynamic_slice x8, local copies, waits for them, and re-layouts, on_device(): lax.map(fill_block, jnp.arange(experts // per_block, dtype=jnp.int32))  4.69 us
    unnamed x9, local copies, waits for them, and re-layouts  2.54 us
  transfers between devices with their start and end apart: 3, of which 1 were waited for; matrix products, arithmetic and copies ran while one was open for 22% of the time, Pallas kernels for 0%

commit v1 on v0

v1 whole, which is shorter than its diff:
```python
import functools

import jax
import jax.numpy as jnp
from jax import lax
from jax.experimental import pallas as pl
from jax.experimental.pallas import tpu as pltpu
from jax.sharding import PartitionSpec as P

balance_weight = 0.5
zloss_weight = 0.02
MESH = pl.DeviceIdType.MESH


def route_grad(logits, cotangent, picks, load):
    levels = lax.broadcasted_iota(jnp.int32, logits.shape, 1)
    expo = jnp.exp(logits)
    total = jnp.sum(expo, axis=1, keepdims=True)
    probs = expo / total
    lse = jnp.log(total)
    first = (picks[:, 0:1] == levels).astype(jnp.float32)
    second = (picks[:, 1:2] == levels).astype(jnp.float32)
    pfirst = jnp.sum(probs * first, axis=1, keepdims=True)
    psecond = jnp.sum(probs * second, axis=1, keepdims=True)
    denom = pfirst + psecond
    gfirst = pfirst / denom
    gsecond = psecond / denom
    cfirst = cotangent[:, 0:1]
    csecond = cotangent[:, 1:2]
    mixed = cfirst * gfirst + csecond * gsecond
    upward = (
        first * (cfirst - mixed) / denom
        + second * (csecond - mixed) / denom
        + balance_weight * load
    )
    inner = jnp.sum(probs * upward, axis=1, keepdims=True)
    grad = probs * (upward - inner) + 2.0 * zloss_weight * lse * probs
    return gfirst, gsecond, grad.astype(jnp.bfloat16)


def flip(index, mask, size):
    out = index
    bit = 1
    while bit < size:
        if mask & bit:
            out = out + bit * (1 - 2 * ((index // bit) % 2))
        bit *= 2
    return out


def exchange(
    n, d, capacity,
    tok_ref, w_ref, cot_ref, pick_ref, slot_ref,
    gates_ref, wgrad_ref, slots_ref,
    lg_send, lg_recv, cnt_send, cnt_recv, own_grad, grads, rows_send, part_send, part_recv, own_wgrad,
    cnt_ss, cnt_rs, lg_ss, lg_rs, gr_ss, gr_rs, a2a_ss, a2a_rs, rs_ss, rs_rs, ag_ss, ag_rs,
):
    me = lax.axis_index("mp")
    my_dp = lax.axis_index("dp")
    rows, feats = tok_ref.shape
    experts = w_ref.shape[1]
    own = rows // n
    half = own // 2
    width = rows_send.shape[1]
    eper = experts // d
    mp_order = list(range(n - 1, 0, -1))
    dp_order = list(range(d - 1, 0, -1))

    def to_mp(k):
        return {"dp": my_dp, "mp": flip(me, k, n)}

    def to_dp(k):
        return {"dp": flip(my_dp, k, d), "mp": me}

    barrier = pltpu.get_barrier_semaphore()
    for k in mp_order:
        pl.semaphore_signal(barrier, inc=1, device_id=to_mp(k), device_id_type=MESH)
    for k in dp_order:
        pl.semaphore_signal(barrier, inc=1, device_id=to_dp(k), device_id_type=MESH)

    partial_value = jnp.dot(tok_ref[...], w_ref[...], preferred_element_type=jnp.float32)
    for p in range(n):
        lo = partial_value[p * own : p * own + half]
        hi = partial_value[p * own + half : (p + 1) * own]
        lg_send[p] = jnp.concatenate([lo, hi], axis=1)
    picks = pick_ref[...]
    levels = lax.broadcasted_iota(jnp.int32, (rows, experts), 1)
    hot = (picks[:, 0:1] == levels).astype(jnp.float32) + (picks[:, 1:2] == levels).astype(jnp.float32)
    local = jnp.sum(hot, axis=0, keepdims=True)
    cnt_send[...] = jnp.broadcast_to(jnp.concatenate([local, local], axis=1), cnt_send.shape)

    pl.semaphore_wait(barrier, n - 1 + d - 1)

    lg = {}
    for k in mp_order:
        lg[k] = pltpu.make_async_remote_copy(
            src_ref=lg_send.at[flip(me, k, n)], dst_ref=lg_recv.at[k],
            send_sem=lg_ss.at[k], recv_sem=lg_rs.at[k], device_id=to_mp(k), device_id_type=MESH)
        lg[k].start()
    cnt = {}
    for k in dp_order:
        cnt[k] = pltpu.make_async_remote_copy(
            src_ref=cnt_send, dst_ref=cnt_recv.at[k],
            send_sem=cnt_ss.at[k], recv_sem=cnt_rs.at[k], device_id=to_dp(k), device_id_type=MESH)
        cnt[k].start()

    slots = slot_ref[...]
    cell = jnp.where(slots >= 0, picks * capacity + slots, -1)
    cell_a = jnp.transpose(jnp.broadcast_to(cell[:, 0:1], (rows, 128)))[:width]
    cell_b = jnp.transpose(jnp.broadcast_to(cell[:, 1:2], (rows, 128)))[:width]
    place = lax.broadcasted_iota(jnp.int32, (width, rows), 0)

    def fill(owner):
        target = place + owner * width
        onehot = ((cell_a == target) | (cell_b == target)).astype(jnp.float32).astype(jnp.bfloat16)
        return jnp.dot(onehot, tok_ref[...], preferred_element_type=jnp.float32).astype(jnp.bfloat16)

    columns = pl.ds(pl.multiple_of(me * feats, feats), feats)
    a2a = {}
    for k in mp_order:
        rows_send[k] = fill(flip(me, k, n))
        a2a[k] = pltpu.make_async_remote_copy(
            src_ref=rows_send.at[k], dst_ref=slots_ref.at[:, columns],
            send_sem=a2a_ss.at[k], recv_sem=a2a_rs.at[k], device_id=to_mp(k), device_id_type=MESH)
        a2a[k].start()
    slots_ref[:, columns] = fill(me)

    for k in dp_order:
        cnt[k].wait()
    counts = cnt_send[...]
    for k in dp_order:
        counts = counts + cnt_recv[k]
    load = counts[0:1, :experts] * experts / (2.0 * rows * d)
    for k in mp_order:
        lg[k].wait()
    packed = lg_send[me]
    for k in mp_order:
        packed = packed + lg_recv[k]
    logits = jnp.concatenate([packed[:, :experts], packed[:, experts:]], axis=0)
    mine = pl.ds(pl.multiple_of(me * own, own), own)
    gfirst, gsecond, grad = route_grad(logits, cot_ref[mine, :], pick_ref[mine, :], load)
    own_grad[...] = grad
    grads[mine, :] = grad
    gr = {}
    for k in mp_order:
        gr[k] = pltpu.make_async_remote_copy(
            src_ref=own_grad, dst_ref=grads.at[mine, :],
            send_sem=gr_ss.at[k], recv_sem=gr_rs.at[k], device_id=to_mp(k), device_id_type=MESH)
        gr[k].start()
    gates_ref[...] = jnp.concatenate([gfirst, gsecond], axis=1)
    for k in mp_order:
        gr[k].wait()

    part = lax.dot_general(
        grads[...], tok_ref[...], (((0,), (0,)), ((), ())), preferred_element_type=jnp.float32)
    for j in range(d):
        part_send[j] = part[j * eper : (j + 1) * eper]
    rs = {}
    for k in dp_order:
        rs[k] = pltpu.make_async_remote_copy(
            src_ref=part_send.at[flip(my_dp, k, d)], dst_ref=part_recv.at[k],
            send_sem=rs_ss.at[k], recv_sem=rs_rs.at[k], device_id=to_dp(k), device_id_type=MESH)
        rs[k].start()
    for k in dp_order:
        rs[k].wait()
    total = part_send[my_dp]
    for k in dp_order:
        total = total + part_recv[k]
    total = total.astype(jnp.bfloat16)
    own_wgrad[...] = total
    wgrad_ref[my_dp] = total
    ag = {}
    for k in dp_order:
        ag[k] = pltpu.make_async_remote_copy(
            src_ref=own_wgrad, dst_ref=wgrad_ref.at[my_dp],
            send_sem=ag_ss.at[k], recv_sem=ag_rs.at[k], device_id=to_dp(k), device_id_type=MESH)
        ag[k].start()
    for k in dp_order:
        ag[k].wait()
    for k in mp_order:
        a2a[k].wait()


def arrange(d, eper, capacity, gates_ref, wgrad_ref, slots_ref, gates_out, wgrad_out, slots_out):
    @pl.when(pl.program_id(0) == 0)
    def _():
        gates_out[...] = gates_ref[...]
        whole = jnp.concatenate([wgrad_ref[j].astype(jnp.float32) for j in range(d)], axis=0)
        wgrad_out[...] = jnp.transpose(whole)

    for e in range(slots_out.shape[1]):
        slots_out[0, e] = slots_ref[e * capacity : (e + 1) * capacity, :]


def on_device(n, d, tokens, router_weight, gate_cotangent, expert_index, slot_index):
    rows, feats = tokens.shape
    experts = router_weight.shape[1]
    own = rows // n
    capacity = 5 * rows // (2 * experts)
    owned = experts // n
    width = owned * capacity
    eper = experts // d
    bf16, f32 = jnp.bfloat16, jnp.float32
    dma = pltpu.SemaphoreType.DMA
    vmem = pl.BlockSpec(memory_space=pltpu.VMEM)
    gates, wgrad, slotted = pl.pallas_call(
        functools.partial(exchange, n, d, capacity),
        out_shape=(
            jax.ShapeDtypeStruct((own, 2), f32),
            jax.ShapeDtypeStruct((d, eper, feats), bf16),
            jax.ShapeDtypeStruct((width, n * feats), bf16),
        ),
        in_specs=[vmem] * 5,
        out_specs=(vmem, vmem, vmem),
        scratch_shapes=[
            pltpu.VMEM((n, own // 2, 2 * experts), f32),
            pltpu.VMEM((n, own // 2, 2 * experts), f32),
            pltpu.VMEM((8, 2 * experts), f32),
            pltpu.VMEM((d, 8, 2 * experts), f32),
            pltpu.VMEM((own, experts), bf16),
            pltpu.VMEM((rows, experts), bf16),
            pltpu.VMEM((n, width, feats), bf16),
            pltpu.VMEM((d, eper, feats), f32),
            pltpu.VMEM((d, eper, feats), f32),
            pltpu.VMEM((eper, feats), bf16),
            dma((d,)), dma((d,)), dma((n,)), dma((n,)), dma((n,)), dma((n,)),
            dma((n,)), dma((n,)), dma((d,)), dma((d,)), dma((d,)), dma((d,)),
        ],
        compiler_params=pltpu.CompilerParams(
            collective_id=0, has_side_effects=True, vmem_limit_bytes=24 * 1024 * 1024
        ),
        name="exchange",
    )(tokens, router_weight, gate_cotangent, expert_index, slot_index)
    steps = 4
    block = n * feats // steps
    gates, router_grad, dispatched = pl.pallas_call(
        functools.partial(arrange, d, eper, capacity),
        grid=(steps,),
        out_shape=(
            jax.ShapeDtypeStruct((own, 2), f32),
            jax.ShapeDtypeStruct((feats, experts), f32),
            jax.ShapeDtypeStruct((1, owned, capacity, n * feats), bf16),
        ),
        in_specs=[
            pl.BlockSpec((own, 2), lambda i: (0, 0)),
            pl.BlockSpec((d, eper, feats), lambda i: (0, 0, 0)),
            pl.BlockSpec((width, block), lambda i: (0, i)),
        ],
        out_specs=(
            pl.BlockSpec((own, 2), lambda i: (0, 0)),
            pl.BlockSpec((feats, experts), lambda i: (0, 0)),
            pl.BlockSpec((1, owned, capacity, block), lambda i: (0, 0, 0, i)),
        ),
        compiler_params=pltpu.CompilerParams(vmem_limit_bytes=16 * 1024 * 1024),
        name="arrange",
    )(gates, wgrad, slotted)
    return gates, router_grad, dispatched


def solution(mesh):
    n, d = mesh.shape["mp"], mesh.shape["dp"]
    in_specs = (P("dp", "mp"), P("mp", None), P("dp", None), P("dp", None), P("dp", None))
    out_specs = (P(("dp", "mp"), None), P("mp", None), P("dp", "mp", None, None))
    return jax.shard_map(
        functools.partial(on_device, n, d),
        mesh=mesh, in_specs=in_specs, out_specs=out_specs, check_vma=False,
    )
```

time: 116 us -> 44.7 us (0.39)
  Pallas kernels: 0 us -> 35.9 us
  waiting for transfers between devices: 33.5 us -> 0 us
  blocking collectives: 26.4 us -> 0 us
  matrix products: 14.1 us -> 0 us
  between operations: 14.1 us -> 0.69 us
  loops' own time: 5.5 us -> 0 us
  starting transfers between devices: 5.38 us -> 0 us
  other arithmetic: 4.94 us -> 0 us
  local copies, waits for them, and re-layouts: 10.8 us -> 7.85 us
    pallas_call x0 -> x2, Pallas kernels: none -> 35.9 us  [the longest x1 35.2 us: on_device(): pl.pallas_call(functools.partial(exchange, n, d, capacity), out_shape=(ja...]
    psum x1 -> x0, waiting for transfers between devices: 33.4 us -> none  [on_device(): router_grad = lax.psum(weight_part, 'dp')]
    all_gather x1 -> x0, blocking collectives: 14.4 us -> none  [on_device(): grad_rows = lax.all_gather(own_grad, 'mp', axis=0, tiled=True)]
    dot_general x10 -> x0, matrix products: 14.1 us -> none  [the longest x8 11.1 us: fill_block(): lax.dot_general(onehot, tokens, (((0,), (0,)), ((), ())), preferred_eleme...]
    psum x1 -> x0, blocking collectives: 12 us -> none  [on_device(): counts = lax.psum(local_counts, 'dp')]
    another operation x1 -> x0, loops' own time: 5.5 us -> none  [on_device(): lax.map(fill_block, jnp.arange(experts // per_block, dtype=jnp.int32))]
    all_to_all x1 -> x0, starting transfers between devices: 5.31 us -> none  [on_device(): lax.all_to_all(slotted, 'mp', split_axis=0, concat_axis=2, tiled=True)]
    dynamic_slice x10 -> x0, local copies, waits for them, and re-layouts: 4.83 us -> none  [the longest x8 4.69 us: on_device(): lax.map(fill_block, jnp.arange(experts // per_block, dtype=jnp.int32))]
  transfers between devices with their start and end apart: 3 -> 0, of which waited for: 1 -> 0; matrix products, arithmetic and copies ran while one was open for 22% -> 0% of each run, Pallas kernels for 0% -> 0%
where the time goes in v1:
time: 44.7 us; the launch traced here: 44.4 us
  Pallas kernels  35.9 us (80%)
  local copies, waits for them, and re-layouts  7.85 us (18%)
  between operations  0.69 us (2%)
    pallas_call x1, Pallas kernels, on_device(): pl.pallas_call(functools.partial(exchange, n, d, capacity), out_shape=(ja...  35.2 us
    unnamed x6, local copies, waits for them, and re-layouts  4.55 us
    pallas_call x3, local copies, waits for them, and re-layouts, on_device(): pl.pallas_call(functools.partial(arrange, d, eper, capacity), grid=(steps...  3.3 us

profile of v1, /device:TPU:0, one launch (start us, length us, event | category | flops | bytes accessed | tf_op | source)
XLA Modules:
  0.0 44.4 jit_solution(496226770120630986)
XLA Ops:
  0.6 0.8 %copy.9.cot_ref = f32[256,2]{1,0:T(8,128)S(1)} copy(f32[256,2]{0,1:T(2,128)} %param.7) | data formatting | bytes 4096 | tf_op args[2]
  1.4 0.8 %copy.10.pick_ref = s32[256,2]{1,0:T(8,128)S(1)} copy(s32[256,2]{0,1:T(2,128)} %param.8) | data formatting | bytes 4096 | tf_op args[3]
  2.3 0.8 %copy.11.slot_ref = s32[256,2]{1,0:T(8,128)S(1)} copy(s32[256,2]{0,1:T(2,128)} %param.9) | data formatting | bytes 4096 | tf_op args[4]
  3.1 1.1 %copy.8.w_ref = bf16[1024,64]{1,0:T(8,128)(2,1)S(1)} copy(bf16[1024,64]{0,1:T(8,128)(2,1)} %param.6) | data formatting | bytes 262144 | tf_op args[1]
  4.2 0.0 copy-start
  4.2 1.0 %copy-done = bf16[256,1024]{1,0:T(8,128)(2,1)S(1)} copy-done((bf16[256,1024]{1,0:T(8,128)(2,1)S(1)}, bf16[256,1024]{1,0:T(8,128)(2,1)}, u32[]{:S(2)}) %copy-start) | copy-done | bytes 524312
  5.2 35.2 %exchange.1 = (f32[32,2]{1,0:T(8,128)S(1)}, bf16[4,16,1024]{2,1,0:T(8,128)(2,1)S(1)}, bf16[80,8192]{1,0:T(8,128)(2,1)S(1)}) custom-call(bf16[256,1024]{1,0:T(8,128)(2,1)S(1)} %copy-done, bf16[1024,64]{1,0:T(8,128)(2,1)S(1)} %copy.8.w_ref, f32[256,2]{1,0:T(8,128)S(1)} %copy.9.cot_ref, s32[256,2]{1,0:T(8,128)S(1)} %copy.10.pick_ref, s32[256,2]{1,0:T(8,128)S(1)} %copy.11.slot_ref), custom_call_target="tpu_custom_call" | custom-call | tf_op jit(solution)/shard_map/exchange/pallas_call | solution.py:206
  40.4 0.7 %arrange.1 = (f32[32,2]{1,0:T(8,128)S(1)}, f32[1024,64]{1,0:T(8,128)S(1)}, bf16[1,8,10,8192]{3,2,1,0:T(8,128)(2,1)S(1)}) custom-call(f32[32,2]{1,0:T(8,128)S(1)} %get-tuple-element.6.gates_ref, bf16[4,16,1024]{2,1,0:T(8,128)(2,1)S(1)} %get-tuple-element.7.wgrad_ref, bf16[80,8192]{1,0:T(8,128)(2,1)S(1)} %get-tuple-element.8.slots_ref), custom_call_target="tpu_custom_call" | custom-call | tf_op jit(solution)/shard_map/arrange/pallas_call | solution.py:236
  41.1 0.6 %copy.12 = f32[32,2]{0,1:T(2,128)} copy(f32[32,2]{1,0:T(8,128)S(1)} %get-tuple-element.9) | data formatting | bytes 512 | tf_op jit(solution)/shard_map/arrange/pallas_call | solution.py:236
  41.8 0.9 %copy.13 = f32[1024,64]{0,1:T(8,128)} copy(f32[1024,64]{1,0:T(8,128)S(1)} %get-tuple-element.10) | data formatting | bytes 524288 | tf_op jit(solution)/shard_map/arrange/pallas_call | solution.py:236
  42.7 1.8 %copy.14 = bf16[1,8,10,8192]{3,1,2,0:T(8,128)(2,1)} copy(bf16[1,8,10,8192]{3,2,1,0:T(8,128)(2,1)S(1)} %get-tuple-element.11) | data formatting | bytes 2621440 | tf_op jit(solution)/shard_map/arrange/pallas_call | solution.py:236
Async XLA Ops:
  4.2 1.0 %copy-start = (bf16[256,1024]{1,0:T(8,128)(2,1)S(1)}, bf16[256,1024]{1,0:T(8,128)(2,1)}, u32[]{:S(2)}) copy-start(bf16[256,1024]{1,0:T(8,128)(2,1)} %tok_ref.1) | copy-start | bytes 1572868

commit v2 on v1

v2 whole, which is shorter than its diff:
```python
import functools

import jax
import jax.numpy as jnp
from jax import lax
from jax.experimental import pallas as pl
from jax.experimental.pallas import tpu as pltpu
from jax.sharding import PartitionSpec as P

balance_weight = 0.5
zloss_weight = 0.02
MESH = pl.DeviceIdType.MESH


def route_grad(logits, cotangent, picks, load):
    levels = lax.broadcasted_iota(jnp.int32, logits.shape, 1).astype(jnp.float32)
    expo = jnp.exp(logits)
    total = jnp.sum(expo, axis=1, keepdims=True)
    probs = expo / total
    lse = jnp.log(total)
    first = (picks[:, 0:1] == levels).astype(jnp.float32)
    second = (picks[:, 1:2] == levels).astype(jnp.float32)
    pfirst = jnp.sum(probs * first, axis=1, keepdims=True)
    psecond = jnp.sum(probs * second, axis=1, keepdims=True)
    denom = pfirst + psecond
    gfirst = pfirst / denom
    gsecond = psecond / denom
    cfirst = cotangent[:, 0:1]
    csecond = cotangent[:, 1:2]
    mixed = cfirst * gfirst + csecond * gsecond
    upward = (
        first * (cfirst - mixed) / denom
        + second * (csecond - mixed) / denom
        + balance_weight * load
    )
    inner = jnp.sum(probs * upward, axis=1, keepdims=True)
    grad = probs * (upward - inner) + 2.0 * zloss_weight * lse * probs
    return gfirst, gsecond, grad.astype(jnp.bfloat16)


def flip(index, mask, size):
    out = index
    bit = 1
    while bit < size:
        if mask & bit:
            out = out + bit * (1 - 2 * ((index // bit) % 2))
        bit *= 2
    return out


def exchange(
    n, d, capacity, owned,
    tok_hbm, w_hbm, cot_ref, pick_ref, slot_ref,
    gates_ref, wgrad_ref, slots_ref,
    tok_ref, w_ref, aux_rows, aux,
    lg_send, lg_recv, cnt_send, cnt_recv, own_grad, grads, rows_send, part_send, part_recv, own_wgrad, wgrads,
    in_sems, cnt_ss, cnt_rs, lg_ss, lg_rs, gr_ss, gr_rs, a2a_ss, a2a_rs, rs_ss, rs_rs, ag_ss, ag_rs,
):
    me = lax.axis_index("mp")
    my_dp = lax.axis_index("dp")
    rows, feats = tok_ref.shape
    experts = w_ref.shape[0]
    own = rows // n
    half = own // 2
    width = owned * capacity
    eper = experts // d
    f32, bf16 = jnp.float32, jnp.bfloat16
    mp_order = list(range(n - 1, 0, -1))
    dp_order = list(range(d - 1, 0, -1))
    early = [k for k in (1, 2, 4) if k < n]
    late = [k for k in mp_order if k not in early]

    def to_mp(k):
        return {"dp": my_dp, "mp": flip(me, k, n)}

    def to_dp(k):
        return {"dp": flip(my_dp, k, d), "mp": me}

    tok_in = pltpu.make_async_copy(tok_hbm, tok_ref, in_sems.at[0])
    w_in = pltpu.make_async_copy(w_hbm, w_ref, in_sems.at[1])
    tok_in.start()
    w_in.start()
    barrier = pltpu.get_barrier_semaphore()
    for k in mp_order:
        pl.semaphore_signal(barrier, inc=1, device_id=to_mp(k), device_id_type=MESH)
    for k in dp_order:
        pl.semaphore_signal(barrier, inc=1, device_id=to_dp(k), device_id_type=MESH)

    picks = pick_ref[...]
    aux_rows[...] = jnp.zeros_like(aux_rows)
    aux_rows[0:2] = picks.astype(f32)
    aux_rows[2:4] = cot_ref[...]
    aux[...] = jnp.transpose(aux_rows[...])
    levels = lax.broadcasted_iota(jnp.int32, (experts, rows), 0)
    hot = (picks[0:1] == levels).astype(f32) + (picks[1:2] == levels).astype(f32)
    local = lax.dot_general(
        jnp.ones((8, rows), bf16), hot.astype(bf16), (((1,), (1,)), ((), ())), preferred_element_type=f32)
    cnt_send[...] = jnp.concatenate([local, local], axis=1)
    slots = slot_ref[...]
    owner_of = lax.div(picks, jnp.int32(owned))
    cell = jnp.where(slots >= 0, owner_of * width + slots * owned + picks - owner_of * owned, -1)
    place = lax.broadcasted_iota(jnp.int32, (width, rows), 0)

    w_in.wait()
    tok_in.wait()
    partial_value = lax.dot_general(
        tok_ref[...], w_ref[...], (((1,), (1,)), ((), ())), preferred_element_type=f32)
    for p in range(n):
        lo = partial_value[p * own : p * own + half]
        hi = partial_value[p * own + half : (p + 1) * own]
        lg_send[p] = jnp.concatenate([lo, hi], axis=1)

    pl.semaphore_wait(barrier, n - 1 + d - 1)

    lg = {}
    for k in mp_order:
        lg[k] = pltpu.make_async_remote_copy(
            src_ref=lg_send.at[flip(me, k, n)], dst_ref=lg_recv.at[k],
            send_sem=lg_ss.at[k], recv_sem=lg_rs.at[k], device_id=to_mp(k), device_id_type=MESH)
        lg[k].start()
    cnt = {}
    for k in dp_order:
        cnt[k] = pltpu.make_async_remote_copy(
            src_ref=cnt_send, dst_ref=cnt_recv.at[k],
            send_sem=cnt_ss.at[k], recv_sem=cnt_rs.at[k], device_id=to_dp(k), device_id_type=MESH)
        cnt[k].start()

    def fill(owner):
        target = place + owner * width
        onehot = ((cell[0:1] == target) | (cell[1:2] == target)).astype(f32).astype(bf16)
        return jnp.dot(onehot, tok_ref[...], preferred_element_type=f32).astype(bf16)

    columns = pl.ds(pl.multiple_of(me * feats, feats), feats)
    a2a = {}

    def push(k):
        a2a[k] = pltpu.make_async_remote_copy(
            src_ref=rows_send.at[k], dst_ref=slots_ref.at[:, columns],
            send_sem=a2a_ss.at[k], recv_sem=a2a_rs.at[k], device_id=to_mp(k), device_id_type=MESH)
        a2a[k].start()

    for k in early:
        rows_send[k] = fill(flip(me, k, n))
        push(k)
    for k in late:
        rows_send[k] = fill(flip(me, k, n))

    for k in dp_order:
        cnt[k].wait()
    counts = cnt_send[...]
    for k in dp_order:
        counts = counts + cnt_recv[k]
    load = counts[0:1, :experts] * experts / (2.0 * rows * d)
    for k in mp_order:
        lg[k].wait()
    packed = lg_send[me]
    for k in mp_order:
        packed = packed + lg_recv[k]
    logits = jnp.concatenate([packed[:, :experts], packed[:, experts:]], axis=0)
    mine = pl.ds(pl.multiple_of(me * own, own), own)
    side = aux[mine, :]
    gfirst, gsecond, grad = route_grad(logits, side[:, 2:4], side[:, 0:2], load)
    own_grad[...] = grad
    grads[mine, :] = grad
    gr = {}
    for k in mp_order:
        gr[k] = pltpu.make_async_remote_copy(
            src_ref=own_grad, dst_ref=grads.at[mine, :],
            send_sem=gr_ss.at[k], recv_sem=gr_rs.at[k], device_id=to_mp(k), device_id_type=MESH)
        gr[k].start()
    for k in late:
        push(k)
    slots_ref[:, columns] = fill(me)
    gates_ref[0:1] = jnp.transpose(jnp.broadcast_to(gfirst, (own, 128)))[0:1]
    gates_ref[1:2] = jnp.transpose(jnp.broadcast_to(gsecond, (own, 128)))[0:1]
    for k in mp_order:
        gr[k].wait()

    part = lax.dot_general(
        grads[...], tok_ref[...], (((0,), (0,)), ((), ())), preferred_element_type=f32)
    for j in range(d):
        part_send[j] = part[j * eper : (j + 1) * eper]
    rs = {}
    for k in dp_order:
        rs[k] = pltpu.make_async_remote_copy(
            src_ref=part_send.at[flip(my_dp, k, d)], dst_ref=part_recv.at[k],
            send_sem=rs_ss.at[k], recv_sem=rs_rs.at[k], device_id=to_dp(k), device_id_type=MESH)
        rs[k].start()
    for k in dp_order:
        rs[k].wait()
    total = part_send[my_dp]
    for k in dp_order:
        total = total + part_recv[k]
    total = total.astype(bf16)
    own_wgrad[...] = total
    wgrads[my_dp] = total
    ag = {}
    for k in dp_order:
        ag[k] = pltpu.make_async_remote_copy(
            src_ref=own_wgrad, dst_ref=wgrads.at[my_dp],
            send_sem=ag_ss.at[k], recv_sem=ag_rs.at[k], device_id=to_dp(k), device_id_type=MESH)
        ag[k].start()
    for k in dp_order:
        ag[k].wait()
    for j in range(d):
        wgrad_ref[j * eper : (j + 1) * eper] = wgrads[j].astype(f32)
    for k in mp_order:
        a2a[k].wait()


def on_device(n, d, tokens, router_weight, gate_cotangent, expert_index, slot_index):
    rows, feats = tokens.shape
    experts = router_weight.shape[1]
    own = rows // n
    capacity = 5 * rows // (2 * experts)
    owned = experts // n
    width = owned * capacity
    eper = experts // d
    bf16, f32 = jnp.bfloat16, jnp.float32
    dma = pltpu.SemaphoreType.DMA
    vmem = pl.BlockSpec(memory_space=pltpu.VMEM)
    hbm = pl.BlockSpec(memory_space=pltpu.HBM)
    gates, wgrad, slotted = pl.pallas_call(
        functools.partial(exchange, n, d, capacity, owned),
        out_shape=(
            jax.ShapeDtypeStruct((2, own), f32),
            jax.ShapeDtypeStruct((experts, feats), f32),
            jax.ShapeDtypeStruct((width, n * feats), bf16),
        ),
        in_specs=[hbm, hbm, vmem, vmem, vmem],
        out_specs=(vmem, vmem, vmem),
        scratch_shapes=[
            pltpu.VMEM((rows, feats), bf16),
            pltpu.VMEM((experts, feats), bf16),
            pltpu.VMEM((8, rows), f32),
            pltpu.VMEM((rows, 8), f32),
            pltpu.VMEM((n, own // 2, 2 * experts), f32),
            pltpu.VMEM((n, own // 2, 2 * experts), f32),
            pltpu.VMEM((8, 2 * experts), f32),
            pltpu.VMEM((d, 8, 2 * experts), f32),
            pltpu.VMEM((own, experts), bf16),
            pltpu.VMEM((rows, experts), bf16),
            pltpu.VMEM((n, width, feats), bf16),
            pltpu.VMEM((d, eper, feats), f32),
            pltpu.VMEM((d, eper, feats), f32),
            pltpu.VMEM((eper, feats), bf16),
            pltpu.VMEM((d, eper, feats), bf16),
            dma((2,)),
            dma((d,)), dma((d,)), dma((n,)), dma((n,)), dma((n,)), dma((n,)),
            dma((n,)), dma((n,)), dma((d,)), dma((d,)), dma((d,)), dma((d,)),
        ],
        compiler_params=pltpu.CompilerParams(
            collective_id=0, has_side_effects=True, vmem_limit_bytes=24 * 1024 * 1024
        ),
        name="exchange",
    )(tokens, router_weight.T, gate_cotangent.T, expert_index.T, slot_index.T)
    dispatched = slotted.reshape(1, capacity, owned, n * feats).transpose(0, 2, 1, 3)
    return gates.T, wgrad.T, dispatched


def solution(mesh):
    n, d = mesh.shape["mp"], mesh.shape["dp"]
    in_specs = (P("dp", "mp"), P("mp", None), P("dp", None), P("dp", None), P("dp", None))
    out_specs = (P(("dp", "mp"), None), P("mp", None), P("dp", "mp", None, None))
    return jax.shard_map(
        functools.partial(on_device, n, d),
        mesh=mesh, in_specs=in_specs, out_specs=out_specs, check_vma=False,
    )
```

time: 44.7 us -> 38.3 us (0.86)
  the two profiles are of different devices: /device:TPU:0 before, /device:TPU:2 now
where the time goes in v2:
time: 38.3 us; the launch traced here: 38 us
  Pallas kernels  31.1 us (81%)
  local copies, waits for them, and re-layouts  6.3 us (16%)
  between operations  0.65 us (2%)
    pallas_call x1, Pallas kernels, on_device(): pl.pallas_call(functools.partial(exchange, n, d, capacity, owned), out_sh...  31.1 us
    unnamed x13, local copies, waits for them, and re-layouts  6.3 us

profile of v2, /device:TPU:2, one launch (start us, length us, event | category | flops | bytes accessed | tf_op | source)
XLA Modules:
  0.0 38.0 jit_solution(1609962011445952288)
XLA Ops:
  0.6 0.0 copy-start
  0.6 1.0 %copy-done = bf16[256,1024]{1,0:T(8,128)(2,1)S(1)} copy-done((bf16[256,1024]{1,0:T(8,128)(2,1)S(1)}, bf16[256,1024]{1,0:T(8,128)(2,1)}, u32[]{:S(2)}) %copy-start) | copy-done | bytes 524312
  1.7 0.0 copy-start.1
  1.7 0.9 %copy-done.1 = bf16[1024,64]{0,1:T(8,128)(2,1)S(1)} copy-done((bf16[1024,64]{0,1:T(8,128)(2,1)S(1)}, bf16[1024,64]{0,1:T(8,128)(2,1)}, u32[]{:S(2)}) %copy-start.1) | copy-done | bytes 131096
  2.6 0.0 copy-start.2
  2.6 0.7 %copy-done.2 = f32[256,2]{0,1:T(2,128)S(1)} copy-done((f32[256,2]{0,1:T(2,128)S(1)}, f32[256,2]{0,1:T(2,128)}, u32[]{:S(2)}) %copy-start.2) | copy-done | bytes 2072
  3.3 0.0 copy-start.3
  3.3 0.7 %copy-done.3 = s32[256,2]{0,1:T(2,128)S(1)} copy-done((s32[256,2]{0,1:T(2,128)S(1)}, s32[256,2]{0,1:T(2,128)}, u32[]{:S(2)}) %copy-start.3) | copy-done | bytes 2072
  3.9 0.0 copy-start.4
  3.9 0.7 %copy-done.4 = s32[256,2]{0,1:T(2,128)S(1)} copy-done((s32[256,2]{0,1:T(2,128)S(1)}, s32[256,2]{0,1:T(2,128)}, u32[]{:S(2)}) %copy-start.4) | copy-done | bytes 2072
  4.6 31.1 %exchange.1 = (f32[2,32]{1,0:T(2,128)S(1)}, f32[64,1024]{1,0:T(8,128)S(1)}, bf16[80,8192]{1,0:T(8,128)(2,1)S(1)}) custom-call(bf16[256,1024]{1,0:T(8,128)(2,1)S(1)} %copy-done, bf16[64,1024]{1,0:T(8,128)(2,1)S(1)} %bitcast.11, f32[2,256]{1,0:T(2,128)S(1)} %bitcast.12, s32[2,256]{1,0:T(2,128)S(1)} %bitcast.13, s32[2,256]{1,0:T(2,128)S(1)} %bitcast.14), custom_call_target="tpu_custom_call" | custom-call | tf_op jit(solution)/shard_map/exchange/pallas_call | solution.py:223
  35.7 0.6 %copy.11 = f32[32,2]{0,1:T(2,128)} copy(f32[32,2]{0,1:T(2,128)S(1)} %bitcast.15) | data formatting | bytes 512
  36.3 0.7 %copy.12 = f32[1024,64]{0,1:T(8,128)} copy(f32[1024,64]{0,1:T(8,128)S(1)} %bitcast.10) | data formatting | bytes 524288
  37.0 1.1 %copy.13 = bf16[1,8,10,8192]{3,1,2,0:T(8,128)(2,1)} copy(bf16[1,8,10,8192]{3,1,2,0:T(8,128)(2,1)S(1)} %bitcast.9) | data formatting | bytes 2621440
Async XLA Ops:
  0.6 1.0 %copy-start = (bf16[256,1024]{1,0:T(8,128)(2,1)S(1)}, bf16[256,1024]{1,0:T(8,128)(2,1)}, u32[]{:S(2)}) copy-start(bf16[256,1024]{1,0:T(8,128)(2,1)} %tok_hbm.1) | copy-start | bytes 1572868
  1.7 0.9 %copy-start.1 = (bf16[1024,64]{0,1:T(8,128)(2,1)S(1)}, bf16[1024,64]{0,1:T(8,128)(2,1)}, u32[]{:S(2)}) copy-start(bf16[1024,64]{0,1:T(8,128)(2,1)} %param.6) | copy-start | bytes 393220
  2.6 0.7 %copy-start.2 = (f32[256,2]{0,1:T(2,128)S(1)}, f32[256,2]{0,1:T(2,128)}, u32[]{:S(2)}) copy-start(f32[256,2]{0,1:T(2,128)} %param.7) | copy-start | bytes 6148
  3.3 0.7 %copy-start.3 = (s32[256,2]{0,1:T(2,128)S(1)}, s32[256,2]{0,1:T(2,128)}, u32[]{:S(2)}) copy-start(s32[256,2]{0,1:T(2,128)} %param.8) | copy-start | bytes 6148
  3.9 0.7 %copy-start.4 = (s32[256,2]{0,1:T(2,128)S(1)}, s32[256,2]{0,1:T(2,128)}, u32[]{:S(2)}) copy-start(s32[256,2]{0,1:T(2,128)} %param.9) | copy-start | bytes 6148

commit v3 on v2

--- a/solution.py
+++ b/solution.py
@@ -50,11 +50,11 @@
 
 def exchange(
     n, d, capacity, owned,
-    tok_hbm, w_hbm, cot_ref, pick_ref, slot_ref,
-    gates_ref, wgrad_ref, slots_ref,
-    tok_ref, w_ref, aux_rows, aux,
+    tok_hbm, w_hbm, cot_hbm, pick_hbm, slot_hbm,
+    gates_hbm, wgrad_hbm, slots_hbm,
+    tok_ref, w_ref, cot_ref, pick_ref, slot_ref, gates_ref, wgrad_ref, aux_rows, aux,
     lg_send, lg_recv, cnt_send, cnt_recv, own_grad, grads, rows_send, part_send, part_recv, own_wgrad, wgrads,
-    in_sems, cnt_ss, cnt_rs, lg_ss, lg_rs, gr_ss, gr_rs, a2a_ss, a2a_rs, rs_ss, rs_rs, ag_ss, ag_rs,
+    in_sems, out_sems, cnt_ss, cnt_rs, lg_ss, lg_rs, gr_ss, gr_rs, a2a_ss, a2a_rs, rs_ss, rs_rs, ag_ss, ag_rs,
 ):
     me = lax.axis_index("mp")
     my_dp = lax.axis_index("dp")
@@ -80,12 +80,21 @@
     w_in = pltpu.make_async_copy(w_hbm, w_ref, in_sems.at[1])
     tok_in.start()
     w_in.start()
+    small_in = [
+        pltpu.make_async_copy(src, dst, in_sems.at[2 + i])
+        for i, (src, dst) in enumerate(
+            ((pick_hbm, pick_ref), (cot_hbm, cot_ref), (slot_hbm, slot_ref)))
+    ]
+    for copy in small_in:
+        copy.start()
     barrier = pltpu.get_barrier_semaphore()
     for k in mp_order:
         pl.semaphore_signal(barrier, inc=1, device_id=to_mp(k), device_id_type=MESH)
     for k in dp_order:
         pl.semaphore_signal(barrier, inc=1, device_id=to_dp(k), device_id_type=MESH)
 
+    for copy in small_in:
+        copy.wait()
     picks = pick_ref[...]
     aux_rows[...] = jnp.zeros_like(aux_rows)
     aux_rows[0:2] = picks.astype(f32)
@@ -135,7 +144,7 @@
 
     def push(k):
         a2a[k] = pltpu.make_async_remote_copy(
-            src_ref=rows_send.at[k], dst_ref=slots_ref.at[:, columns],
+            src_ref=rows_send.at[k], dst_ref=slots_hbm.at[:, columns],
             send_sem=a2a_ss.at[k], recv_sem=a2a_rs.at[k], device_id=to_mp(k), device_id_type=MESH)
         a2a[k].start()
 
@@ -168,9 +177,9 @@
             src_ref=own_grad, dst_ref=grads.at[mine, :],
             send_sem=gr_ss.at[k], recv_sem=gr_rs.at[k], device_id=to_mp(k), device_id_type=MESH)
         gr[k].start()
-    for k in late:
-        push(k)
-    slots_ref[:, columns] = fill(me)
+    rows_send[0] = fill(me)
+    kept = pltpu.make_async_copy(rows_send.at[0], slots_hbm.at[:, columns], out_sems.at[0])
+    kept.start()
     gates_ref[0:1] = jnp.transpose(jnp.broadcast_to(gfirst, (own, 128)))[0:1]
     gates_ref[1:2] = jnp.transpose(jnp.broadcast_to(gsecond, (own, 128)))[0:1]
     for k in mp_order:
@@ -186,6 +195,10 @@
             src_ref=part_send.at[flip(my_dp, k, d)], dst_ref=part_recv.at[k],
             send_sem=rs_ss.at[k], recv_sem=rs_rs.at[k], device_id=to_dp(k), device_id_type=MESH)
         rs[k].start()
+    for k in late:
+        push(k)
+    gates_out = pltpu.make_async_copy(gates_ref, gates_hbm, out_sems.at[1])
+    gates_out.start()
     for k in dp_order:
         rs[k].wait()
     total = part_send[my_dp]
@@ -204,8 +217,28 @@
         ag[k].wait()
     for j in range(d):
         wgrad_ref[j * eper : (j + 1) * eper] = wgrads[j].astype(f32)
+    wgrad_out = pltpu.make_async_copy(wgrad_ref, wgrad_hbm, out_sems.at[2])
+    wgrad_out.start()
     for k in mp_order:
         a2a[k].wait()
+    kept.wait()
+    gates_out.wait()
+    wgrad_out.wait()
+
+
+def hand_out(pieces, gates_ref, wgrad_ref, slots_ref, gates_out, wgrad_out, slots_out, sems):
+    size = slots_ref.shape[0] // pieces
+    copies = [
+        pltpu.make_async_copy(
+            slots_ref.at[pl.ds(i * size, size)], slots_out.at[pl.ds(i * size, size)], sems.at[i])
+        for i in range(pieces)
+    ]
+    copies.append(pltpu.make_async_copy(wgrad_ref, wgrad_out, sems.at[pieces]))
+    copies.append(pltpu.make_async_copy(gates_ref, gates_out, sems.at[pieces + 1]))
+    for copy in copies:
+        copy.start()
+    for copy in copies:
+        copy.wait()
 
 
 def on_device(n, d, tokens, router_weight, gate_cotangent, expert_index, slot_index):
@@ -218,20 +251,25 @@
     eper = experts // d
     bf16, f32 = jnp.bfloat16, jnp.float32
     dma = pltpu.SemaphoreType.DMA
-    vmem = pl.BlockSpec(memory_space=pltpu.VMEM)
     hbm = pl.BlockSpec(memory_space=pltpu.HBM)
+    results = (
+        jax.ShapeDtypeStruct((2, own), f32),
+        jax.ShapeDtypeStruct((experts, feats), f32),
+        jax.ShapeDtypeStruct((width, n * feats), bf16),
+    )
     gates, wgrad, slotted = pl.pallas_call(
         functools.partial(exchange, n, d, capacity, owned),
-        out_shape=(
-            jax.ShapeDtypeStruct((2, own), f32),
-            jax.ShapeDtypeStruct((experts, feats), f32),
-            jax.ShapeDtypeStruct((width, n * feats), bf16),
-        ),
-        in_specs=[hbm, hbm, vmem, vmem, vmem],
-        out_specs=(vmem, vmem, vmem),
+        out_shape=results,
+        in_specs=[hbm] * 5,
+        out_specs=(hbm,) * 3,
         scratch_shapes=[
             pltpu.VMEM((rows, feats), bf16),
             pltpu.VMEM((experts, feats), bf16),
+            pltpu.VMEM((2, rows), f32),
+            pltpu.VMEM((2, rows), jnp.int32),
+            pltpu.VMEM((2, rows), jnp.int32),
+            pltpu.VMEM((2, own), f32),
+            pltpu.VMEM((experts, feats), f32),
             pltpu.VMEM((8, rows), f32),
             pltpu.VMEM((rows, 8), f32),
             pltpu.VMEM((n, own // 2, 2 * experts), f32),
@@ -245,15 +283,25 @@
             pltpu.VMEM((d, eper, feats), f32),
             pltpu.VMEM((eper, feats), bf16),
             pltpu.VMEM((d, eper, feats), bf16),
-            dma((2,)),
+            dma((5,)), dma((3,)),
             dma((d,)), dma((d,)), dma((n,)), dma((n,)), dma((n,)), dma((n,)),
             dma((n,)), dma((n,)), dma((d,)), dma((d,)), dma((d,)), dma((d,)),
         ],
         compiler_params=pltpu.CompilerParams(
-            collective_id=0, has_side_effects=True, vmem_limit_bytes=24 * 1024 * 1024
+            collective_id=0, has_side_effects=True, vmem_limit_bytes=60 * 1024 * 1024
         ),
         name="exchange",
     )(tokens, router_weight.T, gate_cotangent.T, expert_index.T, slot_index.T)
+    pieces = width // 16
+    gates, wgrad, slotted = pl.pallas_call(
+        functools.partial(hand_out, pieces),
+        out_shape=results,
+        in_specs=[hbm] * 3,
+        out_specs=(hbm,) * 3,
+        scratch_shapes=[dma((pieces + 2,))],
+        compiler_params=pltpu.CompilerParams(vmem_limit_bytes=60 * 1024 * 1024),
+        name="hand_out",
+    )(gates, wgrad, slotted)
     dispatched = slotted.reshape(1, capacity, owned, n * feats).transpose(0, 2, 1, 3)
     return gates.T, wgrad.T, dispatched
 

time: 38.3 us -> 75.4 us (1.97)
  the two profiles are of different devices: /device:TPU:2 before, /device:TPU:0 now
where the time goes in v3:
time: 75.4 us; the launch traced here: 75.3 us
  Pallas kernels  74.6 us (99%)
    pallas_call x1, Pallas kernels, on_device(): pl.pallas_call(functools.partial(hand_out, pieces), out_shape=results, in...  48.8 us
    pallas_call x1, Pallas kernels, on_device(): pl.pallas_call(functools.partial(exchange, n, d, capacity, owned), out_sh...  25.8 us

profile of v3, /device:TPU:0, one launch (start us, length us, event | category | flops | bytes accessed | tf_op | source)
XLA Modules:
  0.0 75.3 jit_solution(1209445881060762398)
XLA Ops:
  0.6 25.8 %exchange.1 = (f32[2,32]{1,0:T(2,128)}, f32[64,1024]{1,0:T(8,128)}, bf16[80,8192]{1,0:T(8,128)(2,1)}) custom-call(bf16[256,1024]{1,0:T(8,128)(2,1)} %tok_hbm.1, bf16[64,1024]{1,0:T(8,128)(2,1)} %bitcast.9, f32[2,256]{1,0:T(2,128)} %bitcast.10, s32[2,256]{1,0:T(2,128)} %bitcast.11, s32[2,256]{1,0:T(2,128)} %bitcast.12), custom_call_target="tpu_custom_call" | custom-call | tf_op jit(solution)/shard_map/exchange/pallas_call | solution.py:260
  26.4 48.8 %hand_out.1 = (f32[2,32]{1,0:T(2,128)}, f32[64,1024]{1,0:T(8,128)}, bf16[80,8192]{1,0:T(8,128)(2,1)}) custom-call(f32[2,32]{1,0:T(2,128)} %get-tuple-element.9.gates_ref, f32[64,1024]{1,0:T(8,128)} %get-tuple-element.10.wgrad_ref, bf16[80,8192]{1,0:T(8,128)(2,1)} %get-tuple-element.11.slots_ref), custom_call_target="tpu_custom_call" | custom-call | tf_op jit(solution)/shard_map/hand_out/pallas_call | solution.py:296

commit v4 on v3

--- a/solution.py
+++ b/solution.py
@@ -67,8 +67,9 @@
     f32, bf16 = jnp.float32, jnp.bfloat16
     mp_order = list(range(n - 1, 0, -1))
     dp_order = list(range(d - 1, 0, -1))
-    early = [k for k in (1, 2, 4) if k < n]
-    late = [k for k in mp_order if k not in early]
+    early = [[k for k in batch if k < n] for batch in ((2, 4), (3, 5))]
+    rest = [k for k in mp_order if not any(k in batch for batch in early)] + [0]
+    late = [rest[i : i + 4] for i in range(0, len(rest), 4)]
 
     def to_mp(k):
         return {"dp": my_dp, "mp": flip(me, k, n)}
@@ -134,10 +135,15 @@
             send_sem=cnt_ss.at[k], recv_sem=cnt_rs.at[k], device_id=to_dp(k), device_id_type=MESH)
         cnt[k].start()
 
-    def fill(owner):
-        target = place + owner * width
-        onehot = ((cell[0:1] == target) | (cell[1:2] == target)).astype(f32).astype(bf16)
-        return jnp.dot(onehot, tok_ref[...], preferred_element_type=f32).astype(bf16)
+    def fill(batch):
+        onehots = []
+        for k in batch:
+            target = place + flip(me, k, n) * width
+            onehots.append(((cell[0:1] == target) | (cell[1:2] == target)).astype(f32))
+        onehot = jnp.concatenate(onehots, axis=0).astype(bf16)
+        placed = jnp.dot(onehot, tok_ref[...], preferred_element_type=f32).astype(bf16)
+        for i, k in enumerate(batch):
+            rows_send[k] = placed[i * width : (i + 1) * width]
 
     columns = pl.ds(pl.multiple_of(me * feats, feats), feats)
     a2a = {}
@@ -148,11 +154,10 @@
             send_sem=a2a_ss.at[k], recv_sem=a2a_rs.at[k], device_id=to_mp(k), device_id_type=MESH)
         a2a[k].start()
 
-    for k in early:
-        rows_send[k] = fill(flip(me, k, n))
-        push(k)
-    for k in late:
-        rows_send[k] = fill(flip(me, k, n))
+    for batch in early:
+        fill(batch)
+        for k in batch:
+            push(k)
 
     for k in dp_order:
         cnt[k].wait()
@@ -177,7 +182,8 @@
             src_ref=own_grad, dst_ref=grads.at[mine, :],
             send_sem=gr_ss.at[k], recv_sem=gr_rs.at[k], device_id=to_mp(k), device_id_type=MESH)
         gr[k].start()
-    rows_send[0] = fill(me)
+    for batch in late:
+        fill(batch)
     kept = pltpu.make_async_copy(rows_send.at[0], slots_hbm.at[:, columns], out_sems.at[0])
     kept.start()
     gates_ref[0:1] = jnp.transpose(jnp.broadcast_to(gfirst, (own, 128)))[0:1]
@@ -195,8 +201,10 @@
             src_ref=part_send.at[flip(my_dp, k, d)], dst_ref=part_recv.at[k],
             send_sem=rs_ss.at[k], recv_sem=rs_rs.at[k], device_id=to_dp(k), device_id_type=MESH)
         rs[k].start()
-    for k in late:
-        push(k)
+    for batch in late:
+        for k in batch:
+            if k:
+                push(k)
     gates_out = pltpu.make_async_copy(gates_ref, gates_hbm, out_sems.at[1])
     gates_out.start()
     for k in dp_order:
@@ -226,19 +234,24 @@
     wgrad_out.wait()
 
 
-def hand_out(pieces, gates_ref, wgrad_ref, slots_ref, gates_out, wgrad_out, slots_out, sems):
+def hand_out(
+    pieces, gates_ref, wgrad_ref, slots_ref, gates_out, wgrad_out, slots_out,
+    gates_buf, wgrad_buf, slots_buf, in_sems, sems,
+):
     size = slots_ref.shape[0] // pieces
-    copies = [
-        pltpu.make_async_copy(
-            slots_ref.at[pl.ds(i * size, size)], slots_out.at[pl.ds(i * size, size)], sems.at[i])
-        for i in range(pieces)
-    ]
-    copies.append(pltpu.make_async_copy(wgrad_ref, wgrad_out, sems.at[pieces]))
-    copies.append(pltpu.make_async_copy(gates_ref, gates_out, sems.at[pieces + 1]))
-    for copy in copies:
+    chunks = [pl.ds(i * size, size) for i in range(pieces)]
+    routes = [(slots_ref.at[c], slots_buf.at[c], slots_out.at[c]) for c in chunks]
+    routes.append((wgrad_ref, wgrad_buf, wgrad_out))
+    routes.append((gates_ref, gates_buf, gates_out))
+    ins = [pltpu.make_async_copy(a, b, in_sems.at[i]) for i, (a, b, _) in enumerate(routes)]
+    outs = [pltpu.make_async_copy(b, c, sems.at[i]) for i, (_, b, c) in enumerate(routes)]
+    for copy in ins:
         copy.start()
-    for copy in copies:
+    for copy, out in zip(ins, outs):
         copy.wait()
+        out.start()
+    for out in outs:
+        out.wait()
 
 
 def on_device(n, d, tokens, router_weight, gate_cotangent, expert_index, slot_index):
@@ -298,7 +311,12 @@
         out_shape=results,
         in_specs=[hbm] * 3,
         out_specs=(hbm,) * 3,
-        scratch_shapes=[dma((pieces + 2,))],
+        scratch_shapes=[
+            pltpu.VMEM((2, own), f32),
+            pltpu.VMEM((experts, feats), f32),
+            pltpu.VMEM((width, n * feats), bf16),
+            dma((pieces + 2,)), dma((pieces + 2,)),
+        ],
         compiler_params=pltpu.CompilerParams(vmem_limit_bytes=60 * 1024 * 1024),
         name="hand_out",
     )(gates, wgrad, slotted)

time: 75.4 us -> 32 us (0.42)
  Pallas kernels: 74.6 us -> 31.2 us
    pallas_call x1, Pallas kernels: 48.8 us -> 2.21 us  [on_device(): pl.pallas_call(functools.partial(hand_out, pieces), out_shape=results, in...]
    pallas_call x1, Pallas kernels: 25.8 us -> 29 us  [on_device(): pl.pallas_call(functools.partial(exchange, n, d, capacity, owned), out_sh...]
where the time goes in v4:
time: 32 us; the launch traced here: 31.9 us
  Pallas kernels  31.2 us (98%)
  between operations  0.64 us (2%)
    pallas_call x1, Pallas kernels, on_device(): pl.pallas_call(functools.partial(exchange, n, d, capacity, owned), out_sh...  29 us
    pallas_call x1, Pallas kernels, on_device(): pl.pallas_call(functools.partial(hand_out, pieces), out_shape=results, in...  2.21 us

profile of v4, /device:TPU:0, one launch (start us, length us, event | category | flops | bytes accessed | tf_op | source)
XLA Modules:
  0.0 31.9 jit_solution(10355205408285521770)
XLA Ops:
  0.6 29.0 %exchange.1 = (f32[2,32]{1,0:T(2,128)}, f32[64,1024]{1,0:T(8,128)}, bf16[80,8192]{1,0:T(8,128)(2,1)}) custom-call(bf16[256,1024]{1,0:T(8,128)(2,1)} %tok_hbm.1, bf16[64,1024]{1,0:T(8,128)(2,1)} %bitcast.9, f32[2,256]{1,0:T(2,128)} %bitcast.10, s32[2,256]{1,0:T(2,128)} %bitcast.11, s32[2,256]{1,0:T(2,128)} %bitcast.12), custom_call_target="tpu_custom_call" | custom-call | tf_op jit(solution)/shard_map/exchange/pallas_call | solution.py:273
  29.6 2.2 %hand_out.1 = (f32[2,32]{1,0:T(2,128)}, f32[64,1024]{1,0:T(8,128)}, bf16[80,8192]{1,0:T(8,128)(2,1)}) custom-call(f32[2,32]{1,0:T(2,128)} %get-tuple-element.9.gates_ref, f32[64,1024]{1,0:T(8,128)} %get-tuple-element.10.wgrad_ref, bf16[80,8192]{1,0:T(8,128)(2,1)} %get-tuple-element.11.slots_ref), custom_call_target="tpu_custom_call" | custom-call | tf_op jit(solution)/shard_map/hand_out/pallas_call | solution.py:309

commit v5 on v4

--- a/solution.py
+++ b/solution.py
@@ -67,9 +67,12 @@
     f32, bf16 = jnp.float32, jnp.bfloat16
     mp_order = list(range(n - 1, 0, -1))
     dp_order = list(range(d - 1, 0, -1))
-    early = [[k for k in batch if k < n] for batch in ((2, 4), (3, 5))]
-    rest = [k for k in mp_order if not any(k in batch for batch in early)] + [0]
+    early, middle = [[k for k in batch if k < n] for batch in ((1, 0), (2, 4))]
+    rest = [k for k in mp_order if k not in early + middle]
     late = [rest[i : i + 4] for i in range(0, len(rest), 4)]
+    halves = part_send.shape[0]
+    wide = feats // halves
+    cuts = tok_ref.shape[0] // 2
 
     def to_mp(k):
         return {"dp": my_dp, "mp": flip(me, k, n)}
@@ -77,10 +80,16 @@
     def to_dp(k):
         return {"dp": flip(my_dp, k, d), "mp": me}
 
-    tok_in = pltpu.make_async_copy(tok_hbm, tok_ref, in_sems.at[0])
     w_in = pltpu.make_async_copy(w_hbm, w_ref, in_sems.at[1])
-    tok_in.start()
     w_in.start()
+    tok_in = [
+        pltpu.make_async_copy(
+            tok_hbm.at[i * cuts : (i + 1) * cuts], tok_ref.at[i * cuts : (i + 1) * cuts],
+            in_sems.at[5 * i])
+        for i in range(2)
+    ]
+    for copy in tok_in:
+        copy.start()
     small_in = [
         pltpu.make_async_copy(src, dst, in_sems.at[2 + i])
         for i, (src, dst) in enumerate(
@@ -112,13 +121,15 @@
     place = lax.broadcasted_iota(jnp.int32, (width, rows), 0)
 
     w_in.wait()
-    tok_in.wait()
-    partial_value = lax.dot_general(
-        tok_ref[...], w_ref[...], (((1,), (1,)), ((), ())), preferred_element_type=f32)
-    for p in range(n):
-        lo = partial_value[p * own : p * own + half]
-        hi = partial_value[p * own + half : (p + 1) * own]
-        lg_send[p] = jnp.concatenate([lo, hi], axis=1)
+    for i, copy in enumerate(tok_in):
+        copy.wait()
+        partial_value = lax.dot_general(
+            tok_ref[i * cuts : (i + 1) * cuts], w_ref[...], (((1,), (1,)), ((), ())),
+            preferred_element_type=f32)
+        for p in range(n // 2):
+            lo = partial_value[p * own : p * own + half]
+            hi = partial_value[p * own + half : (p + 1) * own]
+            lg_send[i * (n // 2) + p] = jnp.concatenate([lo, hi], axis=1)
 
     pl.semaphore_wait(barrier, n - 1 + d - 1)
 
@@ -154,10 +165,14 @@
             send_sem=a2a_ss.at[k], recv_sem=a2a_rs.at[k], device_id=to_mp(k), device_id_type=MESH)
         a2a[k].start()
 
-    for batch in early:
-        fill(batch)
-        for k in batch:
+    fill(early)
+    for k in early:
+        if k:
             push(k)
+    kept = pltpu.make_async_copy(rows_send.at[0], slots_hbm.at[:, columns], out_sems.at[0])
+    kept.start()
+    if middle:
+        fill(middle)
 
     for k in dp_order:
         cnt[k].wait()
@@ -182,49 +197,53 @@
             src_ref=own_grad, dst_ref=grads.at[mine, :],
             send_sem=gr_ss.at[k], recv_sem=gr_rs.at[k], device_id=to_mp(k), device_id_type=MESH)
         gr[k].start()
+    for k in middle:
+        push(k)
     for batch in late:
         fill(batch)
-    kept = pltpu.make_async_copy(rows_send.at[0], slots_hbm.at[:, columns], out_sems.at[0])
-    kept.start()
     gates_ref[0:1] = jnp.transpose(jnp.broadcast_to(gfirst, (own, 128)))[0:1]
     gates_ref[1:2] = jnp.transpose(jnp.broadcast_to(gsecond, (own, 128)))[0:1]
     for k in mp_order:
         gr[k].wait()
 
-    part = lax.dot_general(
-        grads[...], tok_ref[...], (((0,), (0,)), ((), ())), preferred_element_type=f32)
-    for j in range(d):
-        part_send[j] = part[j * eper : (j + 1) * eper]
-    rs = {}
-    for k in dp_order:
-        rs[k] = pltpu.make_async_remote_copy(
-            src_ref=part_send.at[flip(my_dp, k, d)], dst_ref=part_recv.at[k],
-            send_sem=rs_ss.at[k], recv_sem=rs_rs.at[k], device_id=to_dp(k), device_id_type=MESH)
-        rs[k].start()
+    rs, ag = {}, {}
+    for h in range(halves):
+        part = lax.dot_general(
+            grads[...], tok_ref[:, h * wide : (h + 1) * wide], (((0,), (0,)), ((), ())),
+            preferred_element_type=f32)
+        for j in range(d):
+            part_send[h, j] = part[j * eper : (j + 1) * eper]
+        for k in dp_order:
+            rs[h, k] = pltpu.make_async_remote_copy(
+                src_ref=part_send.at[h, flip(my_dp, k, d)], dst_ref=part_recv.at[h, k],
+                send_sem=rs_ss.at[h, k], recv_sem=rs_rs.at[h, k],
+                device_id=to_dp(k), device_id_type=MESH)
+            rs[h, k].start()
     for batch in late:
         for k in batch:
-            if k:
-                push(k)
+            push(k)
     gates_out = pltpu.make_async_copy(gates_ref, gates_hbm, out_sems.at[1])
     gates_out.start()
-    for k in dp_order:
-        rs[k].wait()
-    total = part_send[my_dp]
-    for k in dp_order:
-        total = total + part_recv[k]
-    total = total.astype(bf16)
-    own_wgrad[...] = total
-    wgrads[my_dp] = total
-    ag = {}
-    for k in dp_order:
-        ag[k] = pltpu.make_async_remote_copy(
-            src_ref=own_wgrad, dst_ref=wgrads.at[my_dp],
-            send_sem=ag_ss.at[k], recv_sem=ag_rs.at[k], device_id=to_dp(k), device_id_type=MESH)
-        ag[k].start()
-    for k in dp_order:
-        ag[k].wait()
-    for j in range(d):
-        wgrad_ref[j * eper : (j + 1) * eper] = wgrads[j].astype(f32)
+    for h in range(halves):
+        for k in dp_order:
+            rs[h, k].wait()
+        total = part_send[h, my_dp]
+        for k in dp_order:
+            total = total + part_recv[h, k]
+        total = total.astype(bf16)
+        own_wgrad[h] = total
+        wgrads[h, my_dp] = total
+        for k in dp_order:
+            ag[h, k] = pltpu.make_async_remote_copy(
+                src_ref=own_wgrad.at[h], dst_ref=wgrads.at[h, my_dp],
+                send_sem=ag_ss.at[h, k], recv_sem=ag_rs.at[h, k],
+                device_id=to_dp(k), device_id_type=MESH)
+            ag[h, k].start()
+    for h in range(halves):
+        for k in dp_order:
+            ag[h, k].wait()
+        for j in range(d):
+            wgrad_ref[j * eper : (j + 1) * eper, h * wide : (h + 1) * wide] = wgrads[h, j].astype(f32)
     wgrad_out = pltpu.make_async_copy(wgrad_ref, wgrad_hbm, out_sems.at[2])
     wgrad_out.start()
     for k in mp_order:
@@ -262,6 +281,7 @@
     owned = experts // n
     width = owned * capacity
     eper = experts // d
+    halves = 2
     bf16, f32 = jnp.bfloat16, jnp.float32
     dma = pltpu.SemaphoreType.DMA
     hbm = pl.BlockSpec(memory_space=pltpu.HBM)
@@ -292,13 +312,13 @@
             pltpu.VMEM((own, experts), bf16),
             pltpu.VMEM((rows, experts), bf16),
             pltpu.VMEM((n, width, feats), bf16),
-            pltpu.VMEM((d, eper, feats), f32),
-            pltpu.VMEM((d, eper, feats), f32),
-            pltpu.VMEM((eper, feats), bf16),
-            pltpu.VMEM((d, eper, feats), bf16),
-            dma((5,)), dma((3,)),
+            pltpu.VMEM((halves, d, eper, feats // halves), f32),
+            pltpu.VMEM((halves, d, eper, feats // halves), f32),
+            pltpu.VMEM((halves, eper, feats // halves), bf16),
+            pltpu.VMEM((halves, d, eper, feats // halves), bf16),
+            dma((6,)), dma((3,)),
             dma((d,)), dma((d,)), dma((n,)), dma((n,)), dma((n,)), dma((n,)),
-            dma((n,)), dma((n,)), dma((d,)), dma((d,)), dma((d,)), dma((d,)),
+            dma((n,)), dma((n,)), dma((halves, d)), dma((halves, d)), dma((halves, d)), dma((halves, d)),
         ],
         compiler_params=pltpu.CompilerParams(
             collective_id=0, has_side_effects=True, vmem_limit_bytes=60 * 1024 * 1024

time: 32 us -> 30.1 us (0.941)
  Pallas kernels: 31.2 us -> 29.3 us
    pallas_call x1, Pallas kernels: 29 us -> 27.1 us  [on_device(): pl.pallas_call(functools.partial(exchange, n, d, capacity, owned), out_sh...]
where the time goes in v5:
time: 30.1 us; the launch traced here: 30 us
  Pallas kernels  29.3 us (97%)
  between operations  0.64 us (2%)
    pallas_call x1, Pallas kernels, on_device(): pl.pallas_call(functools.partial(exchange, n, d, capacity, owned), out_sh...  27.1 us
    pallas_call x1, Pallas kernels, on_device(): pl.pallas_call(functools.partial(hand_out, pieces), out_shape=results, in...  2.21 us

profile of v5, /device:TPU:0, one launch (start us, length us, event | category | flops | bytes accessed | tf_op | source)
XLA Modules:
  0.0 30.0 jit_solution(5571296078472906790)
XLA Ops:
  0.6 27.1 %exchange.1 = (f32[2,32]{1,0:T(2,128)}, f32[64,1024]{1,0:T(8,128)}, bf16[80,8192]{1,0:T(8,128)(2,1)}) custom-call(bf16[256,1024]{1,0:T(8,128)(2,1)} %tok_hbm.1, bf16[64,1024]{1,0:T(8,128)(2,1)} %bitcast.9, f32[2,256]{1,0:T(2,128)} %bitcast.10, s32[2,256]{1,0:T(2,128)} %bitcast.11, s32[2,256]{1,0:T(2,128)} %bitcast.12), custom_call_target="tpu_custom_call" | custom-call | tf_op jit(solution)/shard_map/exchange/pallas_call | solution.py:293
  27.8 2.2 %hand_out.1 = (f32[2,32]{1,0:T(2,128)}, f32[64,1024]{1,0:T(8,128)}, bf16[80,8192]{1,0:T(8,128)(2,1)}) custom-call(f32[2,32]{1,0:T(2,128)} %get-tuple-element.9.gates_ref, f32[64,1024]{1,0:T(8,128)} %get-tuple-element.10.wgrad_ref, bf16[80,8192]{1,0:T(8,128)(2,1)} %get-tuple-element.11.slots_ref), custom_call_target="tpu_custom_call" | custom-call | tf_op jit(solution)/shard_map/hand_out/pallas_call | solution.py:329

commit v6 on v5

--- a/solution.py
+++ b/solution.py
@@ -51,8 +51,8 @@
 def exchange(
     n, d, capacity, owned,
     tok_hbm, w_hbm, cot_hbm, pick_hbm, slot_hbm,
-    gates_hbm, wgrad_hbm, slots_hbm,
-    tok_ref, w_ref, cot_ref, pick_ref, slot_ref, gates_ref, wgrad_ref, aux_rows, aux,
+    gates_ref, wgrad_ref, slots_ref,
+    tok_ref, w_ref, cot_ref, pick_ref, slot_ref, aux_rows, aux,
     lg_send, lg_recv, cnt_send, cnt_recv, own_grad, grads, rows_send, part_send, part_recv, own_wgrad, wgrads,
     in_sems, out_sems, cnt_ss, cnt_rs, lg_ss, lg_rs, gr_ss, gr_rs, a2a_ss, a2a_rs, rs_ss, rs_rs, ag_ss, ag_rs,
 ):
@@ -67,7 +67,8 @@
     f32, bf16 = jnp.float32, jnp.bfloat16
     mp_order = list(range(n - 1, 0, -1))
     dp_order = list(range(d - 1, 0, -1))
-    early, middle = [[k for k in batch if k < n] for batch in ((1, 0), (2, 4))]
+    early = [k for k in (1, 2, 4, 0) if k < n]
+    middle = [k for k in mp_order if k not in early][:2]
     rest = [k for k in mp_order if k not in early + middle]
     late = [rest[i : i + 4] for i in range(0, len(rest), 4)]
     halves = part_send.shape[0]
@@ -161,7 +162,7 @@
 
     def push(k):
         a2a[k] = pltpu.make_async_remote_copy(
-            src_ref=rows_send.at[k], dst_ref=slots_hbm.at[:, columns],
+            src_ref=rows_send.at[k], dst_ref=slots_ref.at[:, columns],
             send_sem=a2a_ss.at[k], recv_sem=a2a_rs.at[k], device_id=to_mp(k), device_id_type=MESH)
         a2a[k].start()
 
@@ -169,10 +170,8 @@
     for k in early:
         if k:
             push(k)
-    kept = pltpu.make_async_copy(rows_send.at[0], slots_hbm.at[:, columns], out_sems.at[0])
+    kept = pltpu.make_async_copy(rows_send.at[0], slots_ref.at[:, columns], out_sems.at[0])
     kept.start()
-    if middle:
-        fill(middle)
 
     for k in dp_order:
         cnt[k].wait()
@@ -197,14 +196,15 @@
             src_ref=own_grad, dst_ref=grads.at[mine, :],
             send_sem=gr_ss.at[k], recv_sem=gr_rs.at[k], device_id=to_mp(k), device_id_type=MESH)
         gr[k].start()
+    for batch in [middle] + late:
+        if batch:
+            fill(batch)
+    gates_ref[0:1] = jnp.transpose(jnp.broadcast_to(gfirst, (own, 128)))[0:1]
+    gates_ref[1:2] = jnp.transpose(jnp.broadcast_to(gsecond, (own, 128)))[0:1]
+    for k in mp_order:
+        gr[k].wait()
     for k in middle:
         push(k)
-    for batch in late:
-        fill(batch)
-    gates_ref[0:1] = jnp.transpose(jnp.broadcast_to(gfirst, (own, 128)))[0:1]
-    gates_ref[1:2] = jnp.transpose(jnp.broadcast_to(gsecond, (own, 128)))[0:1]
-    for k in mp_order:
-        gr[k].wait()
 
     rs, ag = {}, {}
     for h in range(halves):
@@ -222,8 +222,6 @@
     for batch in late:
         for k in batch:
             push(k)
-    gates_out = pltpu.make_async_copy(gates_ref, gates_hbm, out_sems.at[1])
-    gates_out.start()
     for h in range(halves):
         for k in dp_order:
             rs[h, k].wait()
@@ -244,33 +242,21 @@
             ag[h, k].wait()
         for j in range(d):
             wgrad_ref[j * eper : (j + 1) * eper, h * wide : (h + 1) * wide] = wgrads[h, j].astype(f32)
-    wgrad_out = pltpu.make_async_copy(wgrad_ref, wgrad_hbm, out_sems.at[2])
-    wgrad_out.start()
     for k in mp_order:
         a2a[k].wait()
     kept.wait()
-    gates_out.wait()
-    wgrad_out.wait()
-
-
-def hand_out(
-    pieces, gates_ref, wgrad_ref, slots_ref, gates_out, wgrad_out, slots_out,
-    gates_buf, wgrad_buf, slots_buf, in_sems, sems,
-):
+
+
+def hand_out(pieces, gates_ref, wgrad_ref, slots_ref, gates_out, wgrad_out, slots_out, sems):
     size = slots_ref.shape[0] // pieces
     chunks = [pl.ds(i * size, size) for i in range(pieces)]
-    routes = [(slots_ref.at[c], slots_buf.at[c], slots_out.at[c]) for c in chunks]
-    routes.append((wgrad_ref, wgrad_buf, wgrad_out))
-    routes.append((gates_ref, gates_buf, gates_out))
-    ins = [pltpu.make_async_copy(a, b, in_sems.at[i]) for i, (a, b, _) in enumerate(routes)]
-    outs = [pltpu.make_async_copy(b, c, sems.at[i]) for i, (_, b, c) in enumerate(routes)]
-    for copy in ins:
+    routes = [(slots_ref.at[c], slots_out.at[c]) for c in chunks]
+    routes += [(wgrad_ref, wgrad_out), (gates_ref, gates_out)]
+    copies = [pltpu.make_async_copy(a, b, sems.at[i]) for i, (a, b) in enumerate(routes)]
+    for copy in copies:
         copy.start()
-    for copy, out in zip(ins, outs):
+    for copy in copies:
         copy.wait()
-        out.start()
-    for out in outs:
-        out.wait()
 
 
 def on_device(n, d, tokens, router_weight, gate_cotangent, expert_index, slot_index):
@@ -284,6 +270,7 @@
     halves = 2
     bf16, f32 = jnp.bfloat16, jnp.float32
     dma = pltpu.SemaphoreType.DMA
+    vmem = pl.BlockSpec(memory_space=pltpu.VMEM)
     hbm = pl.BlockSpec(memory_space=pltpu.HBM)
     results = (
         jax.ShapeDtypeStruct((2, own), f32),
@@ -294,15 +281,13 @@
         functools.partial(exchange, n, d, capacity, owned),
         out_shape=results,
         in_specs=[hbm] * 5,
-        out_specs=(hbm,) * 3,
+        out_specs=(vmem,) * 3,
         scratch_shapes=[
             pltpu.VMEM((rows, feats), bf16),
             pltpu.VMEM((experts, feats), bf16),
             pltpu.VMEM((2, rows), f32),
             pltpu.VMEM((2, rows), jnp.int32),
             pltpu.VMEM((2, rows), jnp.int32),
-            pltpu.VMEM((2, own), f32),
-            pltpu.VMEM((experts, feats), f32),
             pltpu.VMEM((8, rows), f32),
             pltpu.VMEM((rows, 8), f32),
             pltpu.VMEM((n, own // 2, 2 * experts), f32),
@@ -316,28 +301,26 @@
             pltpu.VMEM((halves, d, eper, feats // halves), f32),
             pltpu.VMEM((halves, eper, feats // halves), bf16),
             pltpu.VMEM((halves, d, eper, feats // halves), bf16),
-            dma((6,)), dma((3,)),
+            dma((6,)), dma((1,)),
             dma((d,)), dma((d,)), dma((n,)), dma((n,)), dma((n,)), dma((n,)),
             dma((n,)), dma((n,)), dma((halves, d)), dma((halves, d)), dma((halves, d)), dma((halves, d)),
         ],
         compiler_params=pltpu.CompilerParams(
-            collective_id=0, has_side_effects=True, vmem_limit_bytes=60 * 1024 * 1024
+            collective_id=0, has_side_effects=True, vmem_limit_bytes=24 * 1024 * 1024
         ),
         name="exchange",
-    )(tokens, router_weight.T, gate_cotangent.T, expert_index.T, slot_index.T)
+    )(*[
+        pltpu.with_memory_space_constraint(x, pltpu.HBM)
+        for x in (tokens, router_weight.T, gate_cotangent.T, expert_index.T, slot_index.T)
+    ])
     pieces = width // 16
     gates, wgrad, slotted = pl.pallas_call(
         functools.partial(hand_out, pieces),
         out_shape=results,
-        in_specs=[hbm] * 3,
+        in_specs=[vmem] * 3,
         out_specs=(hbm,) * 3,
-        scratch_shapes=[
-            pltpu.VMEM((2, own), f32),
-            pltpu.VMEM((experts, feats), f32),
-            pltpu.VMEM((width, n * feats), bf16),
-            dma((pieces + 2,)), dma((pieces + 2,)),
-        ],
-        compiler_params=pltpu.CompilerParams(vmem_limit_bytes=60 * 1024 * 1024),
+        scratch_shapes=[dma((pieces + 2,))],
+        compiler_params=pltpu.CompilerParams(vmem_limit_bytes=16 * 1024 * 1024),
         name="hand_out",
     )(gates, wgrad, slotted)
     dispatched = slotted.reshape(1, capacity, owned, n * feats).transpose(0, 2, 1, 3)

time: 30.1 us -> 28.5 us (0.947)
  Pallas kernels: 29.3 us -> 27.7 us
    pallas_call x1, Pallas kernels: 2.21 us -> 1.2 us  [on_device(): pl.pallas_call(functools.partial(hand_out, pieces), out_shape=results, in...]
    pallas_call x1, Pallas kernels: 27.1 us -> 26.5 us  [on_device(): pl.pallas_call(functools.partial(exchange, n, d, capacity, owned), out_sh...]
where the time goes in v6:
time: 28.5 us; the launch traced here: 28.3 us
  Pallas kernels  27.7 us (97%)
  between operations  0.64 us (2%)
    pallas_call x1, Pallas kernels, on_device(): pl.pallas_call(functools.partial(exchange, n, d, capacity, owned), out_sh...  26.5 us
    pallas_call x1, Pallas kernels, on_device(): pl.pallas_call(functools.partial(hand_out, pieces), out_shape=results, in...  1.2 us

profile of v6, /device:TPU:0, one launch (start us, length us, event | category | flops | bytes accessed | tf_op | source)
XLA Modules:
  0.0 28.3 jit_solution(9338406599590335604)
XLA Ops:
  0.6 26.5 %exchange.1 = (f32[2,32]{1,0:T(2,128)S(1)}, f32[64,1024]{1,0:T(8,128)S(1)}, bf16[80,8192]{1,0:T(8,128)(2,1)S(1)}) custom-call(bf16[256,1024]{1,0:T(8,128)(2,1)} %tok_hbm.1, bf16[64,1024]{1,0:T(8,128)(2,1)} %bitcast.9, f32[2,256]{1,0:T(2,128)} %bitcast.10, s32[2,256]{1,0:T(2,128)} %bitcast.11, s32[2,256]{1,0:T(2,128)} %bitcast.12), custom_call_target="tpu_custom_call" | custom-call | tf_op jit(solution)/shard_map/exchange/pallas_call | solution.py:280
  27.1 1.2 %hand_out.1 = (f32[2,32]{1,0:T(2,128)}, f32[64,1024]{1,0:T(8,128)}, bf16[80,8192]{1,0:T(8,128)(2,1)}) custom-call(f32[2,32]{1,0:T(2,128)S(1)} %get-tuple-element.9.gates_ref, f32[64,1024]{1,0:T(8,128)S(1)} %get-tuple-element.10.wgrad_ref, bf16[80,8192]{1,0:T(8,128)(2,1)S(1)} %get-tuple-element.11.slots_ref), custom_call_target="tpu_custom_call" | custom-call | tf_op jit(solution)/shard_map/hand_out/pallas_call | solution.py:317

commit v7 on v6

--- a/solution.py
+++ b/solution.py
@@ -53,7 +53,7 @@
     tok_hbm, w_hbm, cot_hbm, pick_hbm, slot_hbm,
     gates_ref, wgrad_ref, slots_ref,
     tok_ref, w_ref, cot_ref, pick_ref, slot_ref, aux_rows, aux,
-    lg_send, lg_recv, cnt_send, cnt_recv, own_grad, grads, rows_send, part_send, part_recv, own_wgrad, wgrads,
+    lg_send, lg_recv, cnt_send, cnt_recv, own_grad, grads, rows_send, part_own, part_send, part_recv, own_wgrad, wgrads,
     in_sems, out_sems, cnt_ss, cnt_rs, lg_ss, lg_rs, gr_ss, gr_rs, a2a_ss, a2a_rs, rs_ss, rs_rs, ag_ss, ag_rs,
 ):
     me = lax.axis_index("mp")
@@ -212,7 +212,8 @@
             grads[...], tok_ref[:, h * wide : (h + 1) * wide], (((0,), (0,)), ((), ())),
             preferred_element_type=f32)
         for j in range(d):
-            part_send[h, j] = part[j * eper : (j + 1) * eper]
+            part_own[h, j] = part[j * eper : (j + 1) * eper]
+            part_send[h, j] = part[j * eper : (j + 1) * eper].astype(bf16)
         for k in dp_order:
             rs[h, k] = pltpu.make_async_remote_copy(
                 src_ref=part_send.at[h, flip(my_dp, k, d)], dst_ref=part_recv.at[h, k],
@@ -225,9 +226,9 @@
     for h in range(halves):
         for k in dp_order:
             rs[h, k].wait()
-        total = part_send[h, my_dp]
-        for k in dp_order:
-            total = total + part_recv[h, k]
+        total = part_own[h, my_dp]
+        for k in dp_order:
+            total = total + part_recv[h, k].astype(f32)
         total = total.astype(bf16)
         own_wgrad[h] = total
         wgrads[h, my_dp] = total
@@ -298,7 +299,8 @@
             pltpu.VMEM((rows, experts), bf16),
             pltpu.VMEM((n, width, feats), bf16),
             pltpu.VMEM((halves, d, eper, feats // halves), f32),
-            pltpu.VMEM((halves, d, eper, feats // halves), f32),
+            pltpu.VMEM((halves, d, eper, feats // halves), bf16),
+            pltpu.VMEM((halves, d, eper, feats // halves), bf16),
             pltpu.VMEM((halves, eper, feats // halves), bf16),
             pltpu.VMEM((halves, d, eper, feats // halves), bf16),
             dma((6,)), dma((1,)),

time: 28.5 us -> 28.5 us (level)
  no operation moved by 1% of the time
where the time goes in v7:
time: 28.5 us; the launch traced here: 28.3 us
  Pallas kernels  27.7 us (97%)
  between operations  0.64 us (2%)
    pallas_call x1, Pallas kernels, on_device(): pl.pallas_call(functools.partial(exchange, n, d, capacity, owned), out_sh...  26.5 us
    pallas_call x1, Pallas kernels, on_device(): pl.pallas_call(functools.partial(hand_out, pieces), out_shape=results, in...  1.2 us

profile of v7, /device:TPU:0, one launch (start us, length us, event | category | flops | bytes accessed | tf_op | source)
XLA Modules:
  0.0 28.3 jit_solution(13181458785444784165)
XLA Ops:
  0.6 26.5 %exchange.1 = (f32[2,32]{1,0:T(2,128)S(1)}, f32[64,1024]{1,0:T(8,128)S(1)}, bf16[80,8192]{1,0:T(8,128)(2,1)S(1)}) custom-call(bf16[256,1024]{1,0:T(8,128)(2,1)} %tok_hbm.1, bf16[64,1024]{1,0:T(8,128)(2,1)} %bitcast.9, f32[2,256]{1,0:T(2,128)} %bitcast.10, s32[2,256]{1,0:T(2,128)} %bitcast.11, s32[2,256]{1,0:T(2,128)} %bitcast.12), custom_call_target="tpu_custom_call" | custom-call | tf_op jit(solution)/shard_map/exchange/pallas_call | solution.py:281
  27.1 1.2 %hand_out.1 = (f32[2,32]{1,0:T(2,128)}, f32[64,1024]{1,0:T(8,128)}, bf16[80,8192]{1,0:T(8,128)(2,1)}) custom-call(f32[2,32]{1,0:T(2,128)S(1)} %get-tuple-element.9.gates_ref, f32[64,1024]{1,0:T(8,128)S(1)} %get-tuple-element.10.wgrad_ref, bf16[80,8192]{1,0:T(8,128)(2,1)S(1)} %get-tuple-element.11.slots_ref), custom_call_target="tpu_custom_call" | custom-call | tf_op jit(solution)/shard_map/hand_out/pallas_call | solution.py:319

commit v8 on v6

--- a/solution.py
+++ b/solution.py
@@ -196,15 +196,16 @@
             src_ref=own_grad, dst_ref=grads.at[mine, :],
             send_sem=gr_ss.at[k], recv_sem=gr_rs.at[k], device_id=to_mp(k), device_id_type=MESH)
         gr[k].start()
-    for batch in [middle] + late:
-        if batch:
-            fill(batch)
     gates_ref[0:1] = jnp.transpose(jnp.broadcast_to(gfirst, (own, 128)))[0:1]
     gates_ref[1:2] = jnp.transpose(jnp.broadcast_to(gsecond, (own, 128)))[0:1]
-    for k in mp_order:
-        gr[k].wait()
+    if middle:
+        fill(middle)
     for k in middle:
         push(k)
+    for batch in late:
+        fill(batch)
+    for k in mp_order:
+        gr[k].wait()
 
     rs, ag = {}, {}
     for h in range(halves):

time: 28.5 us -> 28.7 us (level)
  Pallas kernels: 27.7 us -> 28 us
where the time goes in v8:
time: 28.7 us; the launch traced here: 28.6 us
  Pallas kernels  28 us (98%)
  between operations  0.64 us (2%)
    pallas_call x1, Pallas kernels, on_device(): pl.pallas_call(functools.partial(exchange, n, d, capacity, owned), out_sh...  26.8 us
    pallas_call x1, Pallas kernels, on_device(): pl.pallas_call(functools.partial(hand_out, pieces), out_shape=results, in...  1.2 us

profile of v8, /device:TPU:0, one launch (start us, length us, event | category | flops | bytes accessed | tf_op | source)
XLA Modules:
  0.0 28.6 jit_solution(8666008836233913812)
XLA Ops:
  0.6 26.8 %exchange.1 = (f32[2,32]{1,0:T(2,128)S(1)}, f32[64,1024]{1,0:T(8,128)S(1)}, bf16[80,8192]{1,0:T(8,128)(2,1)S(1)}) custom-call(bf16[256,1024]{1,0:T(8,128)(2,1)} %tok_hbm.1, bf16[64,1024]{1,0:T(8,128)(2,1)} %bitcast.9, f32[2,256]{1,0:T(2,128)} %bitcast.10, s32[2,256]{1,0:T(2,128)} %bitcast.11, s32[2,256]{1,0:T(2,128)} %bitcast.12), custom_call_target="tpu_custom_call" | custom-call | tf_op jit(solution)/shard_map/exchange/pallas_call | solution.py:281
  27.4 1.2 %hand_out.1 = (f32[2,32]{1,0:T(2,128)}, f32[64,1024]{1,0:T(8,128)}, bf16[80,8192]{1,0:T(8,128)(2,1)}) custom-call(f32[2,32]{1,0:T(2,128)S(1)} %get-tuple-element.9.gates_ref, f32[64,1024]{1,0:T(8,128)S(1)} %get-tuple-element.10.wgrad_ref, bf16[80,8192]{1,0:T(8,128)(2,1)S(1)} %get-tuple-element.11.slots_ref), custom_call_target="tpu_custom_call" | custom-call | tf_op jit(solution)/shard_map/hand_out/pallas_call | solution.py:318

commit v9 on v8

--- a/solution.py
+++ b/solution.py
@@ -68,7 +68,7 @@
     mp_order = list(range(n - 1, 0, -1))
     dp_order = list(range(d - 1, 0, -1))
     early = [k for k in (1, 2, 4, 0) if k < n]
-    middle = [k for k in mp_order if k not in early][:2]
+    middle = [k for k in mp_order if k not in early][:3]
     rest = [k for k in mp_order if k not in early + middle]
     late = [rest[i : i + 4] for i in range(0, len(rest), 4)]
     halves = part_send.shape[0]

time: 28.7 us -> 33.2 us (1.16)
  the two profiles are of different devices: /device:TPU:0 before, /device:TPU:10 now
where the time goes in v9:
time: 33.2 us; the launch traced here: 33.1 us
  Pallas kernels  32.5 us (98%)
  between operations  0.64 us (2%)
    pallas_call x1, Pallas kernels, on_device(): pl.pallas_call(functools.partial(exchange, n, d, capacity, owned), out_sh...  31.3 us
    pallas_call x1, Pallas kernels, on_device(): pl.pallas_call(functools.partial(hand_out, pieces), out_shape=results, in...  1.2 us

profile of v9, /device:TPU:10, one launch (start us, length us, event | category | flops | bytes accessed | tf_op | source)
XLA Modules:
  0.0 33.1 jit_solution(306722288530593223)
XLA Ops:
  0.6 31.3 %exchange.1 = (f32[2,32]{1,0:T(2,128)S(1)}, f32[64,1024]{1,0:T(8,128)S(1)}, bf16[80,8192]{1,0:T(8,128)(2,1)S(1)}) custom-call(bf16[256,1024]{1,0:T(8,128)(2,1)} %tok_hbm.1, bf16[64,1024]{1,0:T(8,128)(2,1)} %bitcast.9, f32[2,256]{1,0:T(2,128)} %bitcast.10, s32[2,256]{1,0:T(2,128)} %bitcast.11, s32[2,256]{1,0:T(2,128)} %bitcast.12), custom_call_target="tpu_custom_call" | custom-call | tf_op jit(solution)/shard_map/exchange/pallas_call | solution.py:281
  31.9 1.2 %hand_out.1 = (f32[2,32]{1,0:T(2,128)}, f32[64,1024]{1,0:T(8,128)}, bf16[80,8192]{1,0:T(8,128)(2,1)}) custom-call(f32[2,32]{1,0:T(2,128)S(1)} %get-tuple-element.9.gates_ref, f32[64,1024]{1,0:T(8,128)S(1)} %get-tuple-element.10.wgrad_ref, bf16[80,8192]{1,0:T(8,128)(2,1)S(1)} %get-tuple-element.11.slots_ref), custom_call_target="tpu_custom_call" | custom-call | tf_op jit(solution)/shard_map/hand_out/pallas_call | solution.py:318
